TPU v7x, 256 devices: a whole 4x4x8 slice. The times are simulated.
256 devices in a mesh: grp: 2 (over x_lo), tile: 128 (over z, y, x_hi, core).
Axes of the slice: x: 4 (x_hi: 2, x_lo: 2; x = x_hi * 2 + x_lo), y: 4, z: 8, core: 2. Of those that a mesh axis runs over, the one named last changes fastest.
Arguments:
- fine_probe: bfloat16 [64, 2621440], P(None, ('grp', 'tile')), may hold values from -6 to 6
- coarse_probe: bfloat16 [64, 8192], P(None, ('grp', 'tile')), may hold values from -6 to 6
- fine_diag: bfloat16 [2621440, 128], P(('grp', 'tile'))
- fine_cond: bfloat16 [2621440, 128], P(('grp', 'tile')), may hold values from -0.5 to 0.5
- fine_nbr: int32 [20480, 128], P(('grp', 'tile')), may hold values from -1 to 19327, as said below
- coarse_diag: bfloat16 [8192, 128], P(('grp', 'tile'))
- coarse_cond: bfloat16 [8192, 128], P(('grp', 'tile')), may hold values from -0.5 to 0.5
- coarse_nbr: int32 [64, 128], replicated, may hold values from -1 to 8063, as said below
Outputs:
- fine_out: bfloat16 [64, 2621440], P(None, ('grp', 'tile'))
- fine_back: float32 [64, 2621440], P(None, ('grp', 'tile'))
- coarse_out: bfloat16 [64, 8192], P(None, ('grp', 'tile'))
- coarse_back: float32 [64, 8192], P(None, ('grp', 'tile'))
Inputs may be any that keep to these rules, and one draw needn't show every extreme that they name: `fine_nbr`: row b concerns fine block b, of device d = b // 80, whose points are fine points 128 b onward. Slots 0 to 63 name coarse points (values below 8192). The others are -1 for a padded slot, or a value 8192 + j with j < 1024 naming the fine point 80 * 128 d - 1024 + j (the last 1024 fine points of the device before it along tile within the same grp index; never for tile index 0), or a value 8192 + 1024 + j naming the fine point 80 * 128 d + j, an earlier point of the same device below 128 * b. `coarse_nbr`: row k lists coarse points of earlier coarse blocks (below 128 * k), or -1 for a padded slot.
All inputs are finite; a program needn't handle non-finite values.
Results may differ from a plain program's by a relative error of at most 0.0055.
Values may be sent and summed in bfloat16 or wider, within the bound.
A program may use at most 128 MiB of HBM per device.

v0:
```python
import jax
import jax.numpy as jnp
from jax import lax
from jax.sharding import PartitionSpec as P

RIM = 1024


def passed_along(value, axis, steps):
    count = lax.axis_size(axis)
    first, last = (max(0, -steps), min(count, count - steps))
    return lax.ppermute(value, axis, [(source, source + steps) for source in range(first, last)])


def on_device(
    fine_probe, coarse_probe, fine_diag, fine_cond, fine_nbr, coarse_diag, coarse_cond, coarse_nbr
):
    probes = fine_probe.shape[0]
    fine_pts = fine_probe.shape[1]
    blocks = fine_nbr.shape[0]
    slot_count = fine_nbr.shape[1]
    block_len = fine_diag.shape[1]
    coarse_dev = coarse_probe.shape[1]
    tile_count = lax.axis_size("tile")
    device = lax.axis_index("grp") * tile_count + lax.axis_index("tile")
    coarse_all = lax.all_gather(coarse_probe, ("grp", "tile"), axis=1, tiled=True)
    coarse_pts = coarse_all.shape[1]
    rim_in = passed_along(fine_probe[:, fine_pts - RIM :], "tile", 1)
    context = jnp.concatenate([coarse_all, rim_in, fine_probe], axis=1)
    context_len = context.shape[1]
    valid = fine_nbr >= 0
    local_index = jnp.where(valid, fine_nbr, 0)
    near_vals = jnp.where(valid[None], context[:, local_index], jnp.zeros((), jnp.bfloat16))
    own_probe = fine_probe.reshape(probes, blocks, block_len)
    block_diag = fine_diag.reshape(blocks, block_len, block_len)
    block_cond = fine_cond.reshape(blocks, block_len, slot_count)
    forward = jnp.einsum("pbq,bkq->pbk", own_probe, block_diag, preferred_element_type=jnp.float32)
    forward = forward + jnp.einsum(
        "pbs,bks->pbk", near_vals, block_cond, preferred_element_type=jnp.float32
    )
    fine_res = forward.astype(jnp.bfloat16)
    back_own = jnp.einsum("pbk,bkq->pbq", fine_res, block_diag, preferred_element_type=jnp.float32)
    back_near = jnp.einsum("pbk,bks->pbs", fine_res, block_cond, preferred_element_type=jnp.float32)
    back_near = jnp.where(valid[None], back_near, jnp.zeros((), jnp.float32))
    totals = jnp.zeros((probes, context_len), jnp.float32).at[:, local_index].add(back_near)
    first_row = device * coarse_dev
    coarse_block = first_row // block_len
    block_points = lax.dynamic_slice_in_dim(coarse_all, coarse_block * block_len, block_len, 1)
    coarse_links = lax.dynamic_index_in_dim(coarse_nbr, coarse_block, 0, keepdims=False)
    coarse_valid = coarse_links >= 0
    coarse_index = jnp.where(coarse_valid, coarse_links, 0)
    coarse_near = jnp.where(
        coarse_valid[None], coarse_all[:, coarse_index], jnp.zeros((), jnp.bfloat16)
    )
    coarse_fwd = jnp.einsum(
        "pq,kq->pk", block_points, coarse_diag, preferred_element_type=jnp.float32
    )
    coarse_fwd = coarse_fwd + jnp.einsum(
        "ps,ks->pk", coarse_near, coarse_cond, preferred_element_type=jnp.float32
    )
    coarse_out = coarse_fwd.astype(jnp.bfloat16)
    coarse_own_back = jnp.einsum(
        "pk,kq->pq", coarse_out, coarse_diag, preferred_element_type=jnp.float32
    )
    coarse_near_back = jnp.einsum(
        "pk,ks->ps", coarse_out, coarse_cond, preferred_element_type=jnp.float32
    )
    coarse_near_back = jnp.where(coarse_valid[None], coarse_near_back, jnp.zeros((), jnp.float32))
    coarse_terms = totals[:, :coarse_pts].at[:, coarse_index].add(coarse_near_back)
    block_terms = lax.dynamic_slice_in_dim(coarse_terms, coarse_block * block_len, block_len, 1)
    coarse_terms = lax.dynamic_update_slice_in_dim(
        coarse_terms, block_terms + coarse_own_back, coarse_block * block_len, 1
    )
    coarse_back = lax.psum_scatter(coarse_terms, ("grp", "tile"), scatter_dimension=1, tiled=True)
    rim_terms = passed_along(
        totals[:, coarse_pts : coarse_pts + RIM].astype(jnp.bfloat16), "tile", -1
    ).astype(jnp.float32)
    fine_back = back_own.reshape(probes, fine_pts) + totals[:, coarse_pts + RIM :]
    fine_back = fine_back.at[:, fine_pts - RIM :].add(rim_terms)
    return (fine_res.reshape(probes, fine_pts), fine_back, coarse_out, coarse_back)


def solution(mesh):
    return jax.shard_map(
        on_device,
        mesh=mesh,
        in_specs=(
            P(None, ("grp", "tile")),
            P(None, ("grp", "tile")),
            P(("grp", "tile"), None),
            P(("grp", "tile"), None),
            P(("grp", "tile"), None),
            P(("grp", "tile"), None),
            P(("grp", "tile"), None),
            P(),
        ),
        out_specs=(
            P(None, ("grp", "tile")),
            P(None, ("grp", "tile")),
            P(None, ("grp", "tile")),
            P(None, ("grp", "tile")),
        ),
        check_vma=False,
    )
```

profile of v0, /device:TPU:128, one launch (start us, length us, event | category | flops | bytes accessed | tf_op | source)
XLA Modules:
  0.0 1879.8 jit_solution(6887659032830086078)
XLA Ops:
  8.0 3.9 copy.21
  12.8 1.9 collective-permute-start
  15.5 5.5 fusion.3
  21.7 4.5 collective-permute-done
  26.2 392.4 %all-gather.2.cloned.1.call-done = bf16[64,8192]{0,1:T(8,128)(2,1)} async-done(((bf16[64,32]{0,1:T(8,128)(2,1)}), bf16[64,8192]{0,1:T(8,128)(2,1)}) %all-gather.2.cloned.1.call-update) | async-done | bytes 1048592 | tf_op jit(solution)/shard_map/all_gather | solution.py:26
  418.6 10.3 pad_maximum_fusion
  428.9 37.6 %gather_fusion = bf16[10240,64]{1,0:T(8,128)(2,1)} fusion(bf16[64,19456]{0,1:T(8,128)(2,1)} %pad_maximum_fusion, s32[10240]{0:T(1024)S(1)} %broadcast_clamp_fusion), kind=kCustom, calls=%fused_computation | custom fusion | bytes 2662400 | tf_op jit(solution)/shard_map/gather | solution.py:33
  466.5 4.0 copy.23
  470.5 4.0 fusion.2
  474.6 2.3 select_bitcast_fusion
  477.7 2.3 convolution_bitcast_fusion
  480.0 5.2 copy.34
  485.2 61.4 %scatter_custom_fusion = f32[64,19456]{0,1:T(8,128)} fusion(s32[10240]{0:T(1024)S(1)} %fusion.13, f32[10240,64]{1,0:T(8,128)} %bitcast.60, f32[]{:T(128)} %constant.62.clone.1), kind=kCustom, calls=%fused_computation.6 | custom fusion | flops 655360 | bytes 4981248 | tf_op jit(solution)/shard_map/scatter-add | solution.py:45
  546.6 4.4 slice.45
  551.1 1.1 slice.51
  552.1 2.5 gather_fusion.1
  556.0 5.4 scatter_fusion
  563.3 5.2 copy.33
  568.6 2.0 collective-permute-start.1
  570.6 6.5 slice_add_fusion
  577.1 1.2 copy_bitcast_fusion
  578.3 1.9 fusion.12
  580.2 5.5 copy.32
  585.8 1287.2 %reduce-scatter.2.cloned.1.call-done = f32[64,32]{0,1:T(8,128)} async-done(((f32[64,8192]{0,1:T(8,128)}), f32[64,32]{0,1:T(8,128)}) %reduce-scatter.2.cloned.1.call-update) | async-done | bytes 8208 | tf_op jit(solution)/shard_map/reduce_scatter | solution.py:74
  (37 shorter events, 7.3 us)
Async XLA Ops:
  7.2 463.3 %copy-start = (bf16[10240,128]{1,0:T(8,128)(2,1)S(1)}, bf16[10240,128]{1,0:T(8,128)(2,1)}, u32[]{:S(2)}) copy-start(bf16[10240,128]{1,0:T(8,128)(2,1)} %param.13) | copy-start | bytes 7864324
  7.2 8.3 copy-start.4
  7.2 411.4 %all-gather.2.cloned.1.call-start = ((), (), s32[]{:S(2)}) async-start(), calls=%async_computation.1 | async-start | bytes 2105344 | tf_op jit(solution)/shard_map/all_gather | solution.py:26
  7.9 1865.1 %reduce-scatter.2.cloned.1.call-start = ((), (), s32[]{:S(2)}) async-start(), calls=%async_computation.2 | async-start | bytes 4210688 | tf_op jit(solution)/shard_map/reduce_scatter | solution.py:74
  12.8 13.4 collective-permute-start
  474.5 2.3 copy-start.1
  474.6 3.2 copy-start.3
  546.6 8.0 copy-start.5
  546.6 8.9 copy-start.7
  555.8 7.6 copy-start.6
  568.6 8.6 copy-start.2
  568.6 9.8 collective-permute-start.1
Sparse Core Ops, SparseCore 0:
  9.9 408.6 all-gather.1
  563.4 1309.4 reduce-scatter.1
where the time goes:
time: 1880 us
  waiting for transfers between devices  1680 us (89%)
  other arithmetic  87 us (5%)
  local copies, waits for them, and re-layouts  74.2 us (4%)
    reduce_scatter x1, waiting for transfers between devices, on_device(): lax.psum_scatter(coarse_terms, ('grp', 'tile'), scatter_dimension=1, tile...  1290 us
    all_gather x1, waiting for transfers between devices, on_device(): lax.all_gather(coarse_probe, ('grp', 'tile'), axis=1, tiled=True)  392 us
    scatter-add x1, other arithmetic, on_device(): jnp.zeros((probes, context_len), jnp.float32).at[:, local_index]  61.4 us
    gather x2, local copies, waits for them, and re-layouts, on_device(): context[:, local_index]  41.6 us
  transfers between devices with their start and end apart: 4, of which 3 were waited for; matrix products, arithmetic and copies ran while one was open for 2% of the time, Pallas kernels for 0%

commit v1 on v0

v1 whole, which is shorter than its diff:
```python
import functools

import jax
import jax.numpy as jnp
from jax import lax
from jax.experimental import pallas as pl
from jax.experimental.pallas import tpu as pltpu
from jax.sharding import PartitionSpec as P

RIM = 1024
WIDE = 256
LANES = 128
MESH = pl.DeviceIdType.MESH
NT = (((1,), (1,)), ((), ()))
NN = (((1,), (0,)), ((), ()))
BF = jnp.bfloat16
F32 = jnp.float32


def place():
    grp, tile = lax.axis_index("grp"), lax.axis_index("tile")
    core = tile % 2
    x_hi = (tile // 2) % 2
    y = (tile // 4) % 4
    z = tile // 16
    return grp, z, y, x_hi, core


def dev(grp, z, y, x_hi, core):
    return (grp, ((z * 4 + y) * 2 + x_hi) * 2 + core)


def near_peers(grp, z, y, x_hi, core):
    group = []
    for step in range(1, 8):
        g1, h1, c1 = step // 4, (step // 2) % 2, step % 2
        group.append(((grp + g1) % 2, (x_hi + h1) % 2, (core + c1) % 2))
    return group


def greet(grp, z, y, x_hi, core, others=()):
    barrier = pltpu.get_barrier_semaphore()
    count = 0
    for g1, h1, c1 in near_peers(grp, z, y, x_hi, core):
        pl.semaphore_signal(barrier, inc=1, device_id=dev(g1, z, y, h1, c1), device_id_type=MESH)
        count += 1
    for step in range(1, 8):
        pl.semaphore_signal(
            barrier, inc=1, device_id=dev(grp, (z + step) % 8, y, x_hi, core), device_id_type=MESH
        )
        count += 1
    for step in range(1, 4):
        pl.semaphore_signal(
            barrier, inc=1, device_id=dev(grp, z, (y + step) % 4, x_hi, core), device_id_type=MESH
        )
        count += 1
    for other in others:
        pl.semaphore_signal(barrier, inc=1, device_id=other, device_id_type=MESH)
        count += 1
    pl.semaphore_wait(barrier, count)


def lane_part(ref_value, which):
    return ref_value[:, which * 32 : which * 32 + 32]


def gather_kernel(shard_ref, fine_ref, all_ref, rim_ref, got, s1, r1, s2, r2, s3, r3, s4, r4, s5, r5):
    grp, z, y, x_hi, core = place()
    tile = lax.axis_index("tile")
    tiles = lax.axis_size("tile")
    right = (grp, (tile + 1) % tiles)
    left = (grp, (tile + tiles - 1) % tiles)
    spot = grp * 4 + x_hi * 2 + core
    wide = shard_ref[...]
    got[spot] = jnp.concatenate([wide] * 4, axis=1)
    greet(grp, z, y, x_hi, core, (left, right))
    first = []
    for k, (g1, h1, c1) in enumerate(near_peers(grp, z, y, x_hi, core)):
        part = got.at[spot, pl.ds(pl.multiple_of(c1 * 32, 32), 32), :]
        copy = pltpu.make_async_remote_copy(
            src_ref=part, dst_ref=part, send_sem=s1.at[k], recv_sem=r1.at[k],
            device_id=dev(g1, z, y, h1, c1), device_id_type=MESH,
        )
        copy.start()
        first.append(copy)
    rim = pltpu.make_async_remote_copy(
        src_ref=fine_ref.at[:, pl.ds(fine_ref.shape[1] - RIM, RIM)], dst_ref=rim_ref,
        send_sem=s5, recv_sem=r5, device_id=right, device_id_type=MESH,
    )
    rim.start()
    for copy in first:
        copy.wait()
    rows = pl.ds(pl.multiple_of(core * 32, 32), 32)
    lane = lax.broadcasted_iota(jnp.int32, (32, LANES), 1) // 32
    y_hi, y_at = y // 2, pl.multiple_of((y % 2) * LANES, LANES)
    for g in range(2):
        chunk = got[g * 4, rows, :].astype(F32)
        for k in range(1, 4):
            chunk = jnp.where(lane == k, got[g * 4 + k, rows, :].astype(F32), chunk)
        all_ref[g, z, y_hi, rows, pl.ds(y_at, LANES)] = chunk.astype(BF)
    lanes = pl.ds(y_at, LANES)
    second = []
    for k in range(7):
        part = all_ref.at[:, z, y_hi, rows, lanes]
        copy = pltpu.make_async_remote_copy(
            src_ref=part, dst_ref=part, send_sem=s2.at[k], recv_sem=r2.at[k],
            device_id=dev(grp, (z + k + 1) % 8, y, x_hi, core), device_id_type=MESH,
        )
        copy.start()
        second.append(copy)
    for copy in second:
        copy.wait()
    part = all_ref.at[:, :, y_hi, rows, lanes]
    third = []
    for k in range(3):
        copy = pltpu.make_async_remote_copy(
            src_ref=part, dst_ref=part, send_sem=s3.at[k], recv_sem=r3.at[k],
            device_id=dev(grp, z, (y + k + 1) % 4, x_hi, core), device_id_type=MESH,
        )
        copy.start()
        third.append(copy)
    swap = []
    sibling = dev(grp, z, y, x_hi, 1 - core)
    for k in range(4):
        if k > 0:
            third[k - 1].wait()
        from_y = (y + 4 - k) % 4
        part = all_ref.at[:, :, from_y // 2, rows, pl.ds(pl.multiple_of((from_y % 2) * LANES, LANES), LANES)]
        copy = pltpu.make_async_remote_copy(
            src_ref=part, dst_ref=part, send_sem=s4.at[k], recv_sem=r4.at[k],
            device_id=sibling, device_id_type=MESH,
        )
        copy.start()
        swap.append(copy)
    for copy in swap:
        copy.wait()
    rim.wait()


def gather_call(coarse_probe, fine_probe):
    vmem = pl.BlockSpec(memory_space=pltpu.VMEM)
    dma = pltpu.SemaphoreType.DMA
    return pl.pallas_call(
        gather_kernel,
        name="coarse_gather",
        out_shape=(
            jax.ShapeDtypeStruct((2, 8, 2, 64, WIDE), BF),
            jax.ShapeDtypeStruct((64, RIM), BF),
        ),
        in_specs=[vmem, pl.BlockSpec(memory_space=pl.ANY)],
        out_specs=(vmem, vmem),
        scratch_shapes=[
            pltpu.VMEM((8, 64, LANES), BF),
            dma((7,)), dma((7,)), dma((7,)), dma((7,)), dma((3,)), dma((3,)), dma((4,)), dma((4,)),
            dma, dma,
        ],
        compiler_params=pltpu.CompilerParams(collective_id=0, has_side_effects=True),
    )(coarse_probe, fine_probe)


def sum_kernel(
    terms_ref, rim_ref, back_ref, rim_out_ref,
    half_out, half_in, acc, y_out, y_in, z_out, z_in, x_out, x_in,
    s1, r1, s2, r2, s3, r3, s4, r4, s5, r5,
):
    grp, z, y, x_hi, core = place()
    tile = lax.axis_index("tile")
    tiles = lax.axis_size("tile")
    right = (grp, (tile + 1) % tiles)
    left = (grp, (tile + tiles - 1) % tiles)
    mine = pl.multiple_of(core * 32, 32)
    other = pl.multiple_of((1 - core) * 32, 32)

    @pl.loop(0, 32)
    def _(k):
        half_out[k] = terms_ref[k, pl.ds(other, 32), :].astype(BF)

    greet(grp, z, y, x_hi, core, (left, right))
    swap = pltpu.make_async_remote_copy(
        src_ref=half_out, dst_ref=half_in, send_sem=s1, recv_sem=r1,
        device_id=dev(grp, z, y, x_hi, 1 - core), device_id_type=MESH,
    )
    swap.start()
    rim = pltpu.make_async_remote_copy(
        src_ref=rim_ref, dst_ref=rim_out_ref, send_sem=s5, recv_sem=r5,
        device_id=left, device_id_type=MESH,
    )
    rim.start()
    swap.wait()

    @pl.loop(0, 16)
    def _(gz):
        for y_hi in range(2):
            k = gz * 2 + y_hi
            total = terms_ref[k, pl.ds(mine, 32), :] + half_in[k].astype(F32)
            for y_lo in range(2):
                piece = total[:, y_lo * LANES : y_lo * LANES + LANES]
                acc[y_hi * 2 + y_lo, gz] = piece
                y_out[y_hi * 2 + y_lo, gz] = piece.astype(BF)

    first = []
    for k in range(3):
        copy = pltpu.make_async_remote_copy(
            src_ref=y_out.at[(y + k + 1) % 4], dst_ref=y_in.at[k], send_sem=s2.at[k], recv_sem=r2.at[k],
            device_id=dev(grp, z, (y + k + 1) % 4, x_hi, core), device_id_type=MESH,
        )
        copy.start()
        first.append(copy)
    for copy in first:
        copy.wait()

    @pl.loop(0, 8)
    def _(zz):
        for g in range(2):
            gz = g * 8 + zz
            total = acc[y, gz]
            for k in range(3):
                total = total + y_in[k, gz].astype(F32)
            acc[y, gz] = total
            z_out[zz, g] = total.astype(BF)

    second = []
    for k in range(7):
        copy = pltpu.make_async_remote_copy(
            src_ref=z_out.at[(z + k + 1) % 8], dst_ref=z_in.at[k], send_sem=s3.at[k], recv_sem=r3.at[k],
            device_id=dev(grp, (z + k + 1) % 8, y, x_hi, core), device_id_type=MESH,
        )
        copy.start()
        second.append(copy)
    for copy in second:
        copy.wait()
    for g in range(2):
        total = acc[y, g * 8 + z]
        for k in range(7):
            total = total + z_in[k, g].astype(F32)
        x_out[g] = total
    third = []
    spot = grp * 4 + x_hi * 2 + core
    for k, (g1, h1, c1) in enumerate(near_peers(grp, z, y, x_hi, core)):
        copy = pltpu.make_async_remote_copy(
            src_ref=x_out.at[g1], dst_ref=x_in.at[spot], send_sem=s4.at[k], recv_sem=r4.at[k],
            device_id=dev(g1, z, y, h1, c1), device_id_type=MESH,
        )
        copy.start()
        third.append(copy)
    x_in[spot] = x_out[grp]
    for copy in third:
        copy.wait()
    which = x_hi * 2 + core
    for half in range(2):
        total = (x_in[half] + x_in[2 + half]) + (x_in[4 + half] + x_in[6 + half])
        part = lane_part(total, 0)
        for k in range(1, 4):
            part = jnp.where(which == k, lane_part(total, k), part)
        back_ref[half * 32 : half * 32 + 32, :] = part
    rim.wait()


def sum_call(terms, rim_terms):
    vmem = pl.BlockSpec(memory_space=pltpu.VMEM)
    dma = pltpu.SemaphoreType.DMA
    return pl.pallas_call(
        sum_kernel,
        name="coarse_sum",
        out_shape=(
            jax.ShapeDtypeStruct((64, 32), F32),
            jax.ShapeDtypeStruct((64, RIM), BF),
        ),
        in_specs=[vmem, vmem],
        out_specs=(vmem, vmem),
        scratch_shapes=[
            pltpu.VMEM((32, 32, WIDE), BF),
            pltpu.VMEM((32, 32, WIDE), BF),
            pltpu.VMEM((4, 16, 32, LANES), F32),
            pltpu.VMEM((4, 16, 32, LANES), BF),
            pltpu.VMEM((3, 16, 32, LANES), BF),
            pltpu.VMEM((8, 2, 32, LANES), BF),
            pltpu.VMEM((7, 2, 32, LANES), BF),
            pltpu.VMEM((2, 32, LANES), F32),
            pltpu.VMEM((8, 32, LANES), F32),
            dma, dma, dma((3,)), dma((3,)), dma((7,)), dma((7,)), dma((7,)), dma((7,)), dma, dma,
        ],
        compiler_params=pltpu.CompilerParams(collective_id=1, has_side_effects=True),
    )(terms, rim_terms)


LO = 8
GROUP = 4


def one_hot(hi):
    spots = lax.broadcasted_iota(jnp.int32, (WIDE, WIDE), 0)
    return jnp.where(spots == hi, jnp.float32(1), jnp.float32(0)).astype(BF)


def dot(a, b, dims):
    return lax.dot_general(a, b, dims, preferred_element_type=F32)


def picked(rows, hot, lo, first, acc):
    found = dot(rows, hot, NN)
    for j in range(LO):
        acc = jnp.where(lo == first + j, found[j * 64 : j * 64 + 64], acc)
    return acc


def spread(terms, lo, first):
    zero = jnp.zeros_like(terms)
    parts = [jnp.where(lo == first + j, terms, zero).astype(BF) for j in range(LO)]
    return jnp.concatenate(parts, axis=0)


def halves(a, b):
    lane = lax.broadcasted_iota(jnp.int32, a.shape, 1)
    low = lane < 64
    return (
        jnp.where(low, a, pltpu.roll(b, 64, 1)),
        jnp.where(low, pltpu.roll(a, 64, 1), b),
    )


def coarse_rows(all_ref, first):
    return jnp.concatenate([all_ref[first + j] for j in range(LO)], axis=0)


def coarse_pick(all_ref, hot, lo):
    acc = jnp.zeros((64, WIDE), F32)
    for m in range(32 // LO):
        acc = picked(coarse_rows(all_ref, m * LO), hot, lo, m * LO, acc)
    return acc


def block_kernel(
    all_ref, rim_ref, fine_ref, nbr_ref, diag_ref, cond_ref, cdiag_ref, ccond_ref, clinks_ref,
    out_ref, back_ref, cout_ref, terms_ref, rim_terms_ref,
    ctx, totals, cterms, clo, chi, own_back,
):
    g = pl.program_id(0)
    steps = pl.num_programs(0)
    block = lax.axis_index("grp") * (lax.axis_size("tile") // 4) + lax.axis_index("tile") // 4
    pts = fine_ref.shape[1]

    @pl.when(g == 0)
    def _():
        ctx[:, 0:RIM] = rim_ref[...]
        ctx[:, RIM : RIM + pts] = fine_ref[...]
        ctx[:, RIM + pts :] = jnp.zeros((64, ctx.shape[1] - RIM - pts), BF)
        totals[...] = jnp.zeros_like(totals)
        links = jnp.concatenate(
            [clinks_ref[pl.ds(block, 1), :], jnp.full((1, LANES), -1, jnp.int32)], axis=1
        )
        lo, hi = links >> 8, links & 255
        near = coarse_pick(all_ref, one_hot(hi), lo)[:, :LANES].astype(BF)
        pair = all_ref[block // 2]
        own = jnp.where(block % 2 == 1, pair[:, LANES:].astype(F32), pair[:, :LANES].astype(F32)).astype(BF)
        res = (dot(own, cdiag_ref[...], NT) + dot(near, ccond_ref[...], NT)).astype(BF)
        cout_ref[...] = res
        own_back[...] = dot(res, cdiag_ref[...], NN)
        terms = dot(res, ccond_ref[...], NN)
        cterms[steps] = jnp.concatenate([terms, jnp.zeros_like(terms)], axis=1)
        clo[steps] = lo
        chi[steps] = hi

    rows = [nbr_ref[pl.ds(g * GROUP + r, 1), :] for r in range(GROUP)]
    c01, f01 = halves(rows[0], rows[1])
    c23, f23 = halves(rows[2], rows[3])
    cidx = jnp.concatenate([c01, c23], axis=1)
    fidx = jnp.concatenate([f01, f23], axis=1) - 8192
    lo_c, hi_c = cidx >> 8, cidx & 255
    lo_f, hi_f = fidx >> 8, fidx & 255
    clo[g] = lo_c
    chi[g] = hi_c
    near_c = coarse_pick(all_ref, one_hot(hi_c), lo_c)
    hot_f = one_hot(hi_f)
    spans = (2 * g + 6 + LO - 1) // LO

    def pick_step(m, acc):
        at = m * (LO * WIDE)
        lhs = jnp.concatenate(
            [ctx[:, pl.ds(pl.multiple_of(at + j * WIDE, WIDE), WIDE)] for j in range(LO)], axis=0
        )
        return picked(lhs, hot_f, lo_f, m * LO, acc)

    near_f = lax.fori_loop(0, spans, pick_step, jnp.zeros((64, WIDE), F32))
    terms_c, terms_f = [], []
    for pair in range(GROUP // 2):
        lanes = slice(pair * LANES, pair * LANES + LANES)
        nears = halves(near_c[:, lanes], near_f[:, lanes])
        backs = []
        for r in range(2):
            at = (pair * 2 + r) * LANES
            own = ctx[:, pl.ds(pl.multiple_of(RIM + g * (GROUP * LANES) + at, LANES), LANES)]
            diag = diag_ref[at : at + LANES, :]
            cond = cond_ref[at : at + LANES, :]
            res = (dot(own, diag, NT) + dot(nears[r].astype(BF), cond, NT)).astype(BF)
            out_ref[:, at : at + LANES] = res
            where_at = pl.ds(pl.multiple_of(RIM + g * (GROUP * LANES) + at, LANES), LANES)
            totals[:, where_at] = totals[:, where_at] + dot(res, diag, NN)
            backs.append(dot(res, cond, NN))
        tc, tf = halves(backs[0], backs[1])
        terms_c.append(tc)
        terms_f.append(tf)
    cterms[g] = jnp.concatenate(terms_c, axis=1)
    fterms = jnp.concatenate(terms_f, axis=1)

    def spread_step(m, carry):
        found = dot(spread(fterms, lo_f, m * LO), hot_f, NT)
        for j in range(LO):
            where_at = pl.ds(pl.multiple_of(m * (LO * WIDE) + j * WIDE, WIDE), WIDE)
            totals[:, where_at] = totals[:, where_at] + found[j * 64 : j * 64 + 64]
        return carry

    lax.fori_loop(0, spans, spread_step, 0)

    @pl.when(g == steps - 1)
    def _():
        back_ref[...] = totals[:, RIM : RIM + pts]
        rim_terms_ref[...] = totals[:, 0:RIM].astype(BF)

        @pl.loop(0, 32 // LO)
        def _(m):
            def add(k, acc):
                return acc + dot(spread(cterms[k], clo[k], m * LO), one_hot(chi[k]), NT)

            acc = lax.fori_loop(0, steps + 1, add, jnp.zeros((LO * 64, WIDE), F32))
            for j in range(LO):
                terms_ref[m * LO + j] = acc[j * 64 : j * 64 + 64]

        odd = block % 2 == 1
        own = own_back[...]
        none = jnp.zeros_like(own)
        terms_ref[block // 2] = terms_ref[block // 2] + jnp.concatenate(
            [jnp.where(odd, none, own), jnp.where(odd, own, none)], axis=1
        )


def block_call(coarse_all, rim, fine_probe, nbr, diag, cond, cdiag, ccond, clinks):
    pts = fine_probe.shape[1]
    steps = nbr.shape[0] // GROUP
    whole = lambda *shape: pl.BlockSpec(shape, lambda g: (0,) * len(shape))
    span = GROUP * LANES
    wide = -(-(RIM + pts) // (LO * WIDE)) * LO * WIDE
    return pl.pallas_call(
        block_kernel,
        name="blocks",
        grid=(steps,),
        out_shape=(
            jax.ShapeDtypeStruct((64, pts), BF),
            jax.ShapeDtypeStruct((64, pts), F32),
            jax.ShapeDtypeStruct((64, 32), BF),
            jax.ShapeDtypeStruct((32, 64, WIDE), F32),
            jax.ShapeDtypeStruct((64, RIM), BF),
        ),
        in_specs=[
            whole(32, 64, WIDE), whole(64, RIM), whole(64, pts), whole(*nbr.shape),
            pl.BlockSpec((span, LANES), lambda g: (g, 0)),
            pl.BlockSpec((span, LANES), lambda g: (g, 0)),
            whole(32, LANES), whole(32, LANES), whole(64, LANES),
        ],
        out_specs=(
            pl.BlockSpec((64, span), lambda g: (0, g)),
            whole(64, pts), whole(64, 32), whole(32, 64, WIDE), whole(64, RIM),
        ),
        scratch_shapes=[
            pltpu.VMEM((64, wide), BF),
            pltpu.VMEM((64, wide), F32),
            pltpu.VMEM((steps + 1, 64, WIDE), F32),
            pltpu.VMEM((steps + 1, 1, WIDE), jnp.int32),
            pltpu.VMEM((steps + 1, 1, WIDE), jnp.int32),
            pltpu.VMEM((64, LANES), F32),
        ],
        compiler_params=pltpu.CompilerParams(vmem_limit_bytes=50 * 1024 * 1024),
    )(coarse_all, rim, fine_probe, nbr, diag, cond, cdiag, ccond, clinks)


def on_device(
    fine_probe, coarse_probe, fine_diag, fine_cond, fine_nbr, coarse_diag, coarse_cond, coarse_nbr
):
    coarse_all, rim = gather_call(coarse_probe, fine_probe)
    fine_out, fine_back, coarse_out, terms, rim_terms = block_call(
        coarse_all.reshape(32, 64, WIDE), rim, fine_probe, fine_nbr, fine_diag, fine_cond,
        coarse_diag, coarse_cond, coarse_nbr,
    )
    coarse_back, rim_in = sum_call(terms, rim_terms)
    last = lax.axis_index("tile") == lax.axis_size("tile") - 1
    rim_in = jnp.where(last, jnp.zeros((), F32), rim_in.astype(F32))
    fine_back = fine_back.at[:, -RIM:].add(rim_in)
    return fine_out, fine_back, coarse_out, coarse_back


def solution(mesh):
    columns, rows = P(None, ("grp", "tile")), P(("grp", "tile"), None)
    return jax.shard_map(
        on_device,
        mesh=mesh,
        in_specs=(columns, columns, rows, rows, rows, rows, rows, P()),
        out_specs=(columns, columns, columns, columns),
        check_vma=False,
    )
```

time: 1880 us -> 171 us (0.09)
  the two profiles are of different devices: /device:TPU:128 before, /device:TPU:1 now
where the time goes in v1:
time: 171 us; the launch traced here: 170 us
  Pallas kernels  158 us (92%)
  local copies, waits for them, and re-layouts  10.5 us (6%)
  other arithmetic  1.72 us (1%)
    pallas_call x1, Pallas kernels, block_call(): pl.pallas_call(block_kernel, name='blocks', grid=(steps,), out_shape=(jax...  99.4 us
    pallas_call x1, Pallas kernels, gather_call(): pl.pallas_call(gather_kernel, name='coarse_gather', out_shape=(jax.ShapeD...  31.7 us
    pallas_call x1, Pallas kernels, sum_call(): pl.pallas_call(sum_kernel, name='coarse_sum', out_shape=(jax.ShapeDtypeSt...  26.3 us
    unnamed x19, local copies, waits for them, and re-layouts  10.5 us

profile of v1, /device:TPU:1, one launch (start us, length us, event | category | flops | bytes accessed | tf_op | source)
XLA Modules:
  0.0 170.4 jit_solution(9287646322950715691)
XLA Ops:
  0.6 1.4 copy.12.shard_ref
  2.0 31.7 %coarse_gather.1 = (bf16[2,8,2,64,256]{4,3,2,1,0:T(8,128)(2,1)}, bf16[64,1024]{1,0:T(8,128)(2,1)}) custom-call(bf16[64,32]{1,0:T(8,128)(2,1)} %copy.12.shard_ref, bf16[64,10240]{1,0:T(8,128)(2,1)} %fine_ref.3), custom_call_target="tpu_custom_call" | custom-call | tf_op jit(solution)/shard_map/coarse_gather/pallas_call | solution.py:143
  33.8 0.0 copy-start
  33.8 1.3 copy-done
  35.1 0.0 copy-start.1
  35.1 1.2 copy-done.1
  36.3 0.0 copy-start.2
  36.3 0.9 copy-done.2
  37.2 0.0 copy-start.4
  37.2 0.8 copy-done.4
  38.0 0.0 copy-start.5
  38.0 0.8 copy-done.5
  38.8 0.0 copy-start.6
  38.8 0.7 copy-done.6
  39.5 0.0 copy-start.7
  39.5 0.7 copy-done.7
  40.2 99.4 %blocks.1 = (bf16[64,10240]{1,0:T(8,128)(2,1)}, f32[64,10240]{1,0:T(8,128)}, bf16[64,32]{1,0:T(8,128)(2,1)S(1)}, f32[32,64,256]{2,1,0:T(8,128)}, bf16[64,1024]{1,0:T(8,128)(2,1)S(1)}) custom-call(bf16[32,64,256]{2,1,0:T(8,128)(2,1)S(1)} %bitcast.1, bf16[64,1024]{1,0:T(8,128)(2,1)S(1)} %copy-done.2, bf16[64,10240]{1,0:T(8,128)(2,1)S(1)} %copy-done, ...), custom_call_target="tpu_custom_call" | custom-call | tf_op jit(solution)/shard_map/blocks/pallas_call | solution.py:443
  139.6 0.0 copy-start.3
  139.6 0.6 copy-done.3
  140.2 26.3 %coarse_sum.1 = (f32[64,32]{1,0:T(8,128)}, bf16[64,1024]{1,0:T(8,128)(2,1)}) custom-call(f32[32,64,256]{2,1,0:T(8,128)} %get-tuple-element.29.terms_ref, bf16[64,1024]{1,0:T(8,128)(2,1)} %copy-done.3), custom_call_target="tpu_custom_call" | custom-call | tf_op jit(solution)/shard_map/coarse_sum/pallas_call | solution.py:262
  166.6 1.7 %add_dynamic-update-slice_fusion = f32[64,10240]{1,0:T(8,128)} fusion(f32[64,10240]{1,0:T(8,128)} %get-tuple-element.28, bf16[64,1024]{1,0:T(8,128)(2,1)} %get-tuple-element.31, pred[]{:T(512)S(6)} %eq.3), kind=kLoop, calls=%fused_computation | loop fusion | flops 196608 | bytes 655361 | tf_op jit(solution)/shard_map/scatter-add | solution.py:487
  168.3 1.4 copy.14
  169.8 0.7 copy.13
Async XLA Ops:
  33.8 1.3 copy-start
  35.1 1.2 copy-start.1
  36.3 0.9 copy-start.2
  37.2 0.8 copy-start.4
  38.0 0.8 copy-start.5
  38.8 0.7 copy-start.6
  39.5 0.7 copy-start.7
  139.6 0.7 copy-start.3

commit v2 on v1

v2 whole, which is shorter than its diff:
```python
import jax
import jax.numpy as jnp
from jax import lax
from jax.experimental import pallas as pl
from jax.experimental.pallas import tpu as pltpu
from jax.sharding import PartitionSpec as P

RIM = 1024
WIDE = 256
LANES = 128
MESH = pl.DeviceIdType.MESH
NT = (((1,), (1,)), ((), ()))
NN = (((1,), (0,)), ((), ()))
TN = (((0,), (0,)), ((), ()))
BF = jnp.bfloat16
F32 = jnp.float32
GROUP = 16
SLOTS = GROUP * 64
PART = 8


def place():
    grp, tile = lax.axis_index("grp"), lax.axis_index("tile")
    core = tile % 2
    x_hi = (tile // 2) % 2
    y = (tile // 4) % 4
    z = tile // 16
    return grp, z, y, x_hi, core


def dev(grp, z, y, x_hi, core):
    return (grp, ((z * 4 + y) * 2 + x_hi) * 2 + core)


def near_peers(grp, z, y, x_hi, core):
    group = []
    for step in range(1, 8):
        g1, h1, c1 = step // 4, (step // 2) % 2, step % 2
        group.append(((grp + g1) % 2, (x_hi + h1) % 2, (core + c1) % 2))
    return group


def greet(grp, z, y, x_hi, core, others=()):
    barrier = pltpu.get_barrier_semaphore()
    count = 0
    for g1, h1, c1 in near_peers(grp, z, y, x_hi, core):
        pl.semaphore_signal(barrier, inc=1, device_id=dev(g1, z, y, h1, c1), device_id_type=MESH)
        count += 1
    for step in range(1, 8):
        pl.semaphore_signal(
            barrier, inc=1, device_id=dev(grp, (z + step) % 8, y, x_hi, core), device_id_type=MESH
        )
        count += 1
    for step in range(1, 4):
        pl.semaphore_signal(
            barrier, inc=1, device_id=dev(grp, z, (y + step) % 4, x_hi, core), device_id_type=MESH
        )
        count += 1
    for other in others:
        pl.semaphore_signal(barrier, inc=1, device_id=other, device_id_type=MESH)
        count += 1
    pl.semaphore_wait(barrier, count)


def gather_kernel(
    shard_ref, fine_ref, nbr_ref, all_ref, near_ref,
    got, ctx, hots, s1, r1, s2, r2, s3, r3, s4, r4, s5, r5, s6,
):
    grp, z, y, x_hi, core = place()
    tile = lax.axis_index("tile")
    tiles = lax.axis_size("tile")
    right = (grp, (tile + 1) % tiles)
    left = (grp, (tile + tiles - 1) % tiles)
    spot = grp * 4 + x_hi * 2 + core
    pts = fine_ref.shape[1]
    groups = nbr_ref.shape[0] // GROUP
    load = pltpu.make_async_copy(fine_ref, ctx.at[:, pl.ds(RIM, pts)], s6)
    load.start()
    lane = lax.broadcasted_iota(jnp.int32, (32, LANES), 1) % 32
    tiled = jnp.where(lane == lax.broadcasted_iota(jnp.int32, (32, LANES), 0), jnp.float32(1), jnp.float32(0))
    got[spot] = dot(shard_ref[...], tiled.astype(BF), TN).astype(BF)
    greet(grp, z, y, x_hi, core, (left, right))
    first = []
    for k, (g1, h1, c1) in enumerate(near_peers(grp, z, y, x_hi, core)):
        part = got.at[spot, pl.ds(pl.multiple_of(c1 * 32, 32), 32), :]
        copy = pltpu.make_async_remote_copy(
            src_ref=part, dst_ref=part, send_sem=s1.at[k], recv_sem=r1.at[k],
            device_id=dev(g1, z, y, h1, c1), device_id_type=MESH,
        )
        copy.start()
        first.append(copy)
    rim = pltpu.make_async_remote_copy(
        src_ref=fine_ref.at[:, pl.ds(pts - RIM, RIM)], dst_ref=ctx.at[:, pl.ds(0, RIM)],
        send_sem=s5, recv_sem=r5, device_id=right, device_id_type=MESH,
    )
    rim.start()
    los = []
    for g in range(groups):
        lo, hi = fine_slots(nbr_ref, g)
        los.append(lo)
        hots[g] = one_hot(hi)
    load.wait()

    def pick_own(g):
        acc = jnp.zeros((64, SLOTS), F32)
        for part in range(g + 1):
            acc = picked(lane_rows(ctx, 4 + part * PART, PART), hots[g], los[g], 4 + part * PART, acc)
        near_ref[g] = acc.astype(BF)

    def pick_rim(g):
        acc = picked(lane_rows(ctx, 0, 4), hots[g], los[g], 0, near_ref[g].astype(F32))
        near_ref[g] = acc.astype(BF)

    pick_own(0)
    pick_own(1)
    for copy in first:
        copy.wait()
    rows = pl.ds(pl.multiple_of(core * 32, 32), 32)
    lane = lax.broadcasted_iota(jnp.int32, (32, LANES), 1) // 32
    y_hi, y_at = y // 2, pl.multiple_of((y % 2) * LANES, LANES)
    for g in range(2):
        chunk = got[g * 4, rows, :].astype(F32)
        for k in range(1, 4):
            chunk = jnp.where(lane == k, got[g * 4 + k, rows, :].astype(F32), chunk)
        all_ref[g, z, y_hi, rows, pl.ds(y_at, LANES)] = chunk.astype(BF)
    lanes = pl.ds(y_at, LANES)
    second = []
    for k in range(7):
        part = all_ref.at[:, z, y_hi, rows, lanes]
        copy = pltpu.make_async_remote_copy(
            src_ref=part, dst_ref=part, send_sem=s2.at[k], recv_sem=r2.at[k],
            device_id=dev(grp, (z + k + 1) % 8, y, x_hi, core), device_id_type=MESH,
        )
        copy.start()
        second.append(copy)
    pick_own(2)
    for copy in second:
        copy.wait()
    part = all_ref.at[:, :, y_hi, rows, lanes]
    third = []
    for k in range(3):
        copy = pltpu.make_async_remote_copy(
            src_ref=part, dst_ref=part, send_sem=s3.at[k], recv_sem=r3.at[k],
            device_id=dev(grp, z, (y + k + 1) % 4, x_hi, core), device_id_type=MESH,
        )
        copy.start()
        third.append(copy)
    swap = []
    sibling = dev(grp, z, y, x_hi, 1 - core)
    for k in range(4):
        if k == 1:
            for g in range(3, groups):
                pick_own(g)
        if k > 0:
            third[k - 1].wait()
        from_y = (y + 4 - k) % 4
        part = all_ref.at[:, :, from_y // 2, rows, pl.ds(pl.multiple_of((from_y % 2) * LANES, LANES), LANES)]
        copy = pltpu.make_async_remote_copy(
            src_ref=part, dst_ref=part, send_sem=s4.at[k], recv_sem=r4.at[k],
            device_id=sibling, device_id_type=MESH,
        )
        copy.start()
        swap.append(copy)
    rim.wait()
    for g in range(groups):
        pick_rim(g)
    for copy in swap:
        copy.wait()


def gather_call(coarse_shard, fine_probe, nbr):
    vmem = pl.BlockSpec(memory_space=pltpu.VMEM)
    dma = pltpu.SemaphoreType.DMA
    groups = nbr.shape[0] // GROUP
    return pl.pallas_call(
        gather_kernel,
        name="coarse_gather",
        out_shape=(
            jax.ShapeDtypeStruct((2, 8, 2, 64, WIDE), BF),
            jax.ShapeDtypeStruct((groups, 64, SLOTS), BF),
        ),
        in_specs=[vmem, pl.BlockSpec(memory_space=pl.ANY), vmem],
        out_specs=(vmem, vmem),
        scratch_shapes=[
            pltpu.VMEM((8, 64, LANES), BF),
            pltpu.VMEM((64, RIM + fine_probe.shape[1]), BF),
            pltpu.VMEM((groups, WIDE, SLOTS), BF),
            dma((7,)), dma((7,)), dma((7,)), dma((7,)), dma((3,)), dma((3,)), dma((4,)), dma((4,)),
            dma, dma, dma,
        ],
        compiler_params=pltpu.CompilerParams(
            collective_id=0, has_side_effects=True, vmem_limit_bytes=60 * 1024 * 1024
        ),
    )(coarse_shard, fine_probe, nbr)


def sum_kernel(
    terms_ref, fterms_ref, nbr_ref, own_ref, back_ref, fine_ref,
    hots, totals, rim_out, rim_in, half_out, half_in, acc, y_out, y_in, z_out, z_in, x_out, x_in,
    s1, r1, s2, r2, s3, r3, s4, r4, s5, r5, s6, s7,
):
    grp, z, y, x_hi, core = place()
    tile = lax.axis_index("tile")
    tiles = lax.axis_size("tile")
    right = (grp, (tile + 1) % tiles)
    left = (grp, (tile + tiles - 1) % tiles)
    mine = pl.multiple_of(core * 32, 32)
    pts = own_ref.shape[1]
    groups = nbr_ref.shape[0] // GROUP
    load = pltpu.make_async_copy(own_ref, totals, s6)
    load.start()
    other = pl.multiple_of((1 - core) * 32, 32)

    @pl.loop(0, 32)
    def _(k):
        half_out[k] = terms_ref[k, pl.ds(other, 32), :].astype(BF)

    greet(grp, z, y, x_hi, core, (left, right))
    swap = pltpu.make_async_remote_copy(
        src_ref=half_out, dst_ref=half_in, send_sem=s1, recv_sem=r1,
        device_id=dev(grp, z, y, x_hi, 1 - core), device_id_type=MESH,
    )
    swap.start()
    los = []
    for g in range(groups):
        lo, hi = fine_slots(nbr_ref, g)
        los.append(lo.astype(BF))
        hots[g] = one_hot(hi)

    def spread_sum(first, parts, start):
        total = None
        for g in range(start, groups):
            found = dot(spread(fterms_ref[g], los[g], first, parts), hots[g], NT)
            total = found if total is None else total + found
        return total

    rim_terms = spread_sum(0, 4, 0)
    for j in range(4):
        rim_out[:, j * WIDE : j * WIDE + WIDE] = rim_terms[j * 64 : j * 64 + 64].astype(BF)
    rim = pltpu.make_async_remote_copy(
        src_ref=rim_out, dst_ref=rim_in, send_sem=s5, recv_sem=r5,
        device_id=left, device_id_type=MESH,
    )
    rim.start()
    stores = []

    def spread_own(part):
        found = spread_sum(4 + part * PART, PART, part)
        for j in range(PART):
            at = (part * PART + j) * WIDE
            totals[:, at : at + WIDE] = totals[:, at : at + WIDE] + found[j * 64 : j * 64 + 64]

    def store_own(part):
        at = pl.ds(part * PART * WIDE, PART * WIDE)
        store = pltpu.make_async_copy(totals.at[:, at], fine_ref.at[:, at], s7.at[part])
        store.start()
        stores.append(store)

    swap.wait()

    @pl.loop(0, 16)
    def _(gz):
        for y_hi in range(2):
            k = gz * 2 + y_hi
            total = terms_ref[k, pl.ds(mine, 32), :] + half_in[k].astype(F32)
            for y_lo in range(2):
                piece = total[:, y_lo * LANES : y_lo * LANES + LANES]
                acc[y_hi * 2 + y_lo, gz] = piece
                y_out[y_hi * 2 + y_lo, gz] = piece.astype(BF)

    first = []
    for k in range(3):
        copy = pltpu.make_async_remote_copy(
            src_ref=y_out.at[(y + k + 1) % 4], dst_ref=y_in.at[k], send_sem=s2.at[k], recv_sem=r2.at[k],
            device_id=dev(grp, z, (y + k + 1) % 4, x_hi, core), device_id_type=MESH,
        )
        copy.start()
        first.append(copy)
    load.wait()
    for part in range(2):
        spread_own(part)
        store_own(part)
    for copy in first:
        copy.wait()

    @pl.loop(0, 8)
    def _(zz):
        for g in range(2):
            gz = g * 8 + zz
            total = acc[y, gz]
            for k in range(3):
                total = total + y_in[k, gz].astype(F32)
            acc[y, gz] = total
            z_out[zz, g] = total.astype(BF)

    second = []
    for k in range(7):
        copy = pltpu.make_async_remote_copy(
            src_ref=z_out.at[(z + k + 1) % 8], dst_ref=z_in.at[k], send_sem=s3.at[k], recv_sem=r3.at[k],
            device_id=dev(grp, (z + k + 1) % 8, y, x_hi, core), device_id_type=MESH,
        )
        copy.start()
        second.append(copy)
    spread_own(2)
    store_own(2)
    for copy in second:
        copy.wait()
    for g in range(2):
        total = acc[y, g * 8 + z]
        for k in range(7):
            total = total + z_in[k, g].astype(F32)
        x_out[g] = total
    third = []
    spot = grp * 4 + x_hi * 2 + core
    for k, (g1, h1, c1) in enumerate(near_peers(grp, z, y, x_hi, core)):
        copy = pltpu.make_async_remote_copy(
            src_ref=x_out.at[g1], dst_ref=x_in.at[spot], send_sem=s4.at[k], recv_sem=r4.at[k],
            device_id=dev(g1, z, y, h1, c1), device_id_type=MESH,
        )
        copy.start()
        third.append(copy)
    x_in[spot] = x_out[grp]
    for part in range(3, groups):
        spread_own(part)
        if part < groups - 1:
            store_own(part)
    rim.wait()
    keep = jnp.where(tile == tiles - 1, jnp.float32(0), jnp.float32(1))
    totals[:, pts - RIM :] = totals[:, pts - RIM :] + rim_in[...].astype(F32) * keep
    store_own(groups - 1)
    for copy in third:
        copy.wait()
    which = x_hi * 2 + core
    total = jnp.concatenate(
        [(x_in[half] + x_in[2 + half]) + (x_in[4 + half] + x_in[6 + half]) for half in range(2)], axis=0
    ).T
    part = total[0:32]
    for k in range(1, 4):
        part = jnp.where(which == k, total[k * 32 : k * 32 + 32], part)
    back_ref[...] = part
    for store in stores:
        store.wait()


def sum_call(terms, fterms, nbr, own_back):
    vmem = pl.BlockSpec(memory_space=pltpu.VMEM)
    away = pl.BlockSpec(memory_space=pl.ANY)
    dma = pltpu.SemaphoreType.DMA
    groups = nbr.shape[0] // GROUP
    return pl.pallas_call(
        sum_kernel,
        name="coarse_sum",
        out_shape=(
            jax.ShapeDtypeStruct((32, 64), F32),
            jax.ShapeDtypeStruct(own_back.shape, F32),
        ),
        in_specs=[vmem, vmem, vmem, away],
        out_specs=(vmem, away),
        scratch_shapes=[
            pltpu.VMEM((groups, WIDE, SLOTS), BF),
            pltpu.VMEM(own_back.shape, F32),
            pltpu.VMEM((64, RIM), BF),
            pltpu.VMEM((64, RIM), BF),
            pltpu.VMEM((32, 32, WIDE), BF),
            pltpu.VMEM((32, 32, WIDE), BF),
            pltpu.VMEM((4, 16, 32, LANES), F32),
            pltpu.VMEM((4, 16, 32, LANES), BF),
            pltpu.VMEM((3, 16, 32, LANES), BF),
            pltpu.VMEM((8, 2, 32, LANES), BF),
            pltpu.VMEM((7, 2, 32, LANES), BF),
            pltpu.VMEM((2, 32, LANES), F32),
            pltpu.VMEM((8, 32, LANES), F32),
            dma, dma, dma((3,)), dma((3,)), dma((7,)), dma((7,)), dma((7,)), dma((7,)), dma, dma, dma,
            dma((groups,)),
        ],
        compiler_params=pltpu.CompilerParams(
            collective_id=1, has_side_effects=True, vmem_limit_bytes=60 * 1024 * 1024
        ),
    )(terms, fterms, nbr, own_back)


def one_hot(hi):
    spots = lax.broadcasted_iota(jnp.int32, (WIDE, hi.shape[1]), 0)
    return jnp.where(spots == hi, jnp.float32(1), jnp.float32(0)).astype(BF)


def dot(a, b, dims):
    return lax.dot_general(a, b, dims, preferred_element_type=F32)


def picked(rows, hot, lo, first, acc):
    found = dot(rows, hot, NN)
    for j in range(found.shape[0] // 64):
        acc = jnp.where(lo == first + j, found[j * 64 : j * 64 + 64], acc)
    return acc


def spread(terms, lo, first, parts):
    zero = jnp.zeros_like(terms)
    return jnp.concatenate([jnp.where(lo == (first + j), terms, zero) for j in range(parts)], axis=0)


def halves(a, b):
    lane = lax.broadcasted_iota(jnp.int32, a.shape, 1)
    low = lane < 64
    return (
        jnp.where(low, a, pltpu.roll(b, 64, 1)),
        jnp.where(low, pltpu.roll(a, 64, 1), b),
    )


def lane_rows(ref, first, parts):
    return jnp.concatenate([ref[:, (first + j) * WIDE : (first + j + 1) * WIDE] for j in range(parts)], axis=0)


def slots(nbr_ref, g, which):
    rows = [nbr_ref[pl.ds(g * GROUP + r, 1), :] for r in range(GROUP)]
    return jnp.concatenate([halves(rows[r], rows[r + 1])[which] for r in range(0, GROUP, 2)], axis=1)


def fine_slots(nbr_ref, g):
    at = slots(nbr_ref, g, 1) - 8192
    return at >> 8, at & 255


def coarse_rows(all_ref, first):
    return jnp.concatenate([all_ref[first + j] for j in range(PART)], axis=0)


def coarse_pick(all_ref, hot, lo):
    acc = jnp.zeros((64, lo.shape[1]), F32)
    for m in range(0, 32, PART):
        acc = picked(coarse_rows(all_ref, m), hot, lo, m, acc)
    return acc


def coarse_spread(terms_ref, terms, lo, hot):
    for m in range(0, 32, PART):
        found = dot(spread(terms, lo, m, PART), hot, NT)
        for j in range(PART):
            terms_ref[m + j] = terms_ref[m + j] + found[j * 64 : j * 64 + 64]


def block_kernel(
    all_ref, near_ref, fine_ref, nbr_ref, diag_ref, cond_ref, cdiag_ref, ccond_ref, clinks_ref,
    out_ref, back_ref, cout_ref, terms_ref, fterms_ref,
):
    g = pl.program_id(0)
    block = lax.axis_index("grp") * (lax.axis_size("tile") // 4) + lax.axis_index("tile") // 4

    @pl.when(g == 0)
    def _():
        terms_ref[...] = jnp.zeros_like(terms_ref)
        links = jnp.concatenate(
            [clinks_ref[pl.ds(block, 1), :], jnp.full((1, LANES), -1, jnp.int32)], axis=1
        )
        lo, hi = links >> 8, links & 255
        hot = one_hot(hi)
        near = coarse_pick(all_ref, hot, lo)[:, :LANES].astype(BF)
        pair = all_ref[block // 2]
        own = jnp.where(block % 2 == 1, pair[:, LANES:].astype(F32), pair[:, :LANES].astype(F32)).astype(BF)
        res = (dot(cdiag_ref[...], own, NT) + dot(ccond_ref[...], near, NT)).astype(BF)
        cout_ref[...] = res
        own = dot(res, cdiag_ref[...], TN)
        terms = dot(res, ccond_ref[...], TN).astype(BF)
        coarse_spread(terms_ref, jnp.concatenate([terms, jnp.zeros_like(terms)], axis=1), lo.astype(BF), hot)
        odd = block % 2 == 1
        none = jnp.zeros_like(own)
        terms_ref[block // 2] = terms_ref[block // 2] + jnp.concatenate(
            [jnp.where(odd, none, own), jnp.where(odd, own, none)], axis=1
        )

    cidx = slots(nbr_ref, g, 0)
    lo_c, hi_c = cidx >> 8, cidx & 255
    hot_c = one_hot(hi_c)
    near_c = coarse_pick(all_ref, hot_c, lo_c).astype(BF)
    near_f = near_ref[...]
    nears, results, backs = [], [], []
    for pair in range(GROUP // 2):
        lanes = slice(pair * LANES, pair * LANES + LANES)
        nears.extend(halves(near_c[:, lanes].astype(F32), near_f[:, lanes].astype(F32)))
    for r in range(GROUP):
        at = r * LANES
        both = jnp.concatenate([diag_ref[at : at + LANES, :], cond_ref[at : at + LANES, :]], axis=1)
        pair = jnp.concatenate([fine_ref[:, at : at + LANES], nears[r].astype(BF)], axis=1)
        results.append(dot(pair, both, NT).astype(BF))
    for r in range(GROUP):
        at = r * LANES
        out_ref[:, at : at + LANES] = results[r]
        both = jnp.concatenate([diag_ref[at : at + LANES, :], cond_ref[at : at + LANES, :]], axis=1)
        back = dot(results[r], both, NN)
        back_ref[:, at : at + LANES] = back[:, :LANES]
        backs.append(back[:, LANES:])
    terms = [halves(backs[r], backs[r + 1]) for r in range(0, GROUP, 2)]
    fterms_ref[...] = jnp.concatenate([pair[1] for pair in terms], axis=1).astype(BF)
    cterms = jnp.concatenate([pair[0] for pair in terms], axis=1).astype(BF)
    coarse_spread(terms_ref, cterms, lo_c.astype(BF), hot_c)


def block_call(coarse_all, near, fine_probe, nbr, diag, cond, cdiag, ccond, clinks):
    pts = fine_probe.shape[1]
    steps = nbr.shape[0] // GROUP
    whole = lambda *shape: pl.BlockSpec(shape, lambda g: (0,) * len(shape))
    span = GROUP * LANES
    columns = pl.BlockSpec((64, span), lambda g: (0, g))
    return pl.pallas_call(
        block_kernel,
        name="blocks",
        grid=(steps,),
        out_shape=(
            jax.ShapeDtypeStruct((64, pts), BF),
            jax.ShapeDtypeStruct((64, pts), F32),
            jax.ShapeDtypeStruct((32, 64), BF),
            jax.ShapeDtypeStruct((32, 64, WIDE), F32),
            jax.ShapeDtypeStruct((steps, 64, SLOTS), BF),
        ),
        in_specs=[
            whole(32, 64, WIDE), pl.BlockSpec((None, 64, SLOTS), lambda g: (g, 0, 0)),
            columns, whole(*nbr.shape),
            pl.BlockSpec((span, LANES), lambda g: (g, 0)),
            pl.BlockSpec((span, LANES), lambda g: (g, 0)),
            whole(32, LANES), whole(32, LANES), whole(64, LANES),
        ],
        out_specs=(
            columns, columns, whole(32, 64), whole(32, 64, WIDE),
            pl.BlockSpec((None, 64, SLOTS), lambda g: (g, 0, 0)),
        ),
        compiler_params=pltpu.CompilerParams(vmem_limit_bytes=60 * 1024 * 1024),
    )(coarse_all, near, fine_probe, nbr, diag, cond, cdiag, ccond, clinks)


def on_device(
    fine_probe, coarse_probe, fine_diag, fine_cond, fine_nbr, coarse_diag, coarse_cond, coarse_nbr
):
    coarse_all, near = gather_call(coarse_probe.T, fine_probe, fine_nbr)
    fine_out, own_back, coarse_out, terms, fine_terms = block_call(
        coarse_all.reshape(32, 64, WIDE), near, fine_probe, fine_nbr, fine_diag, fine_cond,
        coarse_diag, coarse_cond, coarse_nbr,
    )
    coarse_back, fine_back = sum_call(terms, fine_terms, fine_nbr, own_back)
    return fine_out, fine_back, coarse_out.T, coarse_back.T


def solution(mesh):
    columns, rows = P(None, ("grp", "tile")), P(("grp", "tile"), None)
    return jax.shard_map(
        on_device,
        mesh=mesh,
        in_specs=(columns, columns, rows, rows, rows, rows, rows, P()),
        out_specs=(columns, columns, columns, columns),
        check_vma=False,
    )
```

time: 171 us -> 84.1 us (0.49)
  Pallas kernels: 158 us -> 79.2 us
  local copies, waits for them, and re-layouts: 10.5 us -> 4.04 us
  other arithmetic: 1.72 us -> 0 us
    pallas_call x1, Pallas kernels: 99.4 us -> 20.2 us  [block_call(): pl.pallas_call(block_kernel, name='blocks', grid=(steps,), out_shape=(jax...]
    unnamed x19 -> x4, local copies, waits for them, and re-layouts: 10.5 us -> 4.04 us
    scatter-add x1 -> x0, other arithmetic: 1.72 us -> none  [on_device(): fine_back = fine_back.at[:, -RIM:].add(rim_in)]
where the time goes in v2:
time: 84.1 us; the launch traced here: 83.9 us
  Pallas kernels  79.2 us (94%)
  local copies, waits for them, and re-layouts  4.04 us (5%)
    pallas_call x1, Pallas kernels, gather_call(): pl.pallas_call(gather_kernel, name='coarse_gather', out_shape=(jax.ShapeD...  32.3 us
    pallas_call x1, Pallas kernels, sum_call(): pl.pallas_call(sum_kernel, name='coarse_sum', out_shape=(jax.ShapeDtypeSt...  26.7 us
    pallas_call x1, Pallas kernels, block_call(): pl.pallas_call(block_kernel, name='blocks', grid=(steps,), out_shape=(jax...  20.2 us
    unnamed x4, local copies, waits for them, and re-layouts  4.04 us

profile of v2, /device:TPU:1, one launch (start us, length us, event | category | flops | bytes accessed | tf_op | source)
XLA Modules:
  0.0 83.9 jit_solution(9878445005117726045)
XLA Ops:
  0.6 32.3 %coarse_gather.1 = (bf16[2,8,2,64,256]{4,3,2,1,0:T(8,128)(2,1)}, bf16[5,64,1024]{2,1,0:T(8,128)(2,1)}) custom-call(bf16[32,64]{1,0:T(8,128)(2,1)} %bitcast.6, bf16[64,10240]{1,0:T(8,128)(2,1)} %fine_ref.3, s32[80,128]{1,0:T(8,128)} %nbr_ref.5), custom_call_target="tpu_custom_call" | custom-call | tf_op jit(solution)/shard_map/coarse_gather/pallas_call | solution.py:175
  32.9 20.2 %blocks.1 = (bf16[64,10240]{1,0:T(8,128)(2,1)}, f32[64,10240]{1,0:T(8,128)}, bf16[32,64]{1,0:T(8,128)(2,1)}, f32[32,64,256]{2,1,0:T(8,128)}, bf16[5,64,1024]{2,1,0:T(8,128)(2,1)}) custom-call(bf16[32,64,256]{2,1,0:T(8,128)(2,1)} %bitcast.4, bf16[5,64,1024]{2,1,0:T(8,128)(2,1)} %get-tuple-element.14.near_ref, bf16[64,10240]{1,0:T(8,128)(2,1)} %fine_ref.3, ...), custom_call_target="tpu_custom_call" | custom-call | tf_op jit(solution)/shard_map/blocks/pallas_call | solution.py:506
  53.1 26.7 %coarse_sum.1 = (f32[32,64]{1,0:T(8,128)}, f32[64,10240]{1,0:T(8,128)}) custom-call(f32[32,64,256]{2,1,0:T(8,128)} %get-tuple-element.16.terms_ref, bf16[5,64,1024]{2,1,0:T(8,128)(2,1)} %get-tuple-element.17.fterms_ref, s32[80,128]{1,0:T(8,128)} %nbr_ref.5, f32[64,10240]{1,0:T(8,128)} %get-tuple-element.18.own_ref), custom_call_target="tpu_custom_call" | custom-call | tf_op jit(solution)/shard_map/coarse_sum/pallas_call | solution.py:350
  79.9 0.0 copy-start
  79.9 3.4 %copy.14 = f32[64,10240]{1,0:T(8,128)} copy(f32[64,10240]{1,0:T(8,128)} %get-tuple-element.27) | data formatting | bytes 5242880
  83.3 0.0 copy-done
  83.3 0.6 copy.15
Async XLA Ops:
  79.9 3.4 %copy-start = (f32[32,64]{1,0:T(8,128)S(1)}, f32[32,64]{1,0:T(8,128)}, u32[]{:S(2)}) copy-start(f32[32,64]{1,0:T(8,128)} %get-tuple-element.21) | copy-start | bytes 24580

commit v3 on v2

v3 whole, which is shorter than its diff:
```python
import jax
import jax.numpy as jnp
from jax import lax
from jax.experimental import pallas as pl
from jax.experimental.pallas import tpu as pltpu
from jax.sharding import PartitionSpec as P

RIM = 1024
WIDE = 256
LANES = 128
MESH = pl.DeviceIdType.MESH
NT = (((1,), (1,)), ((), ()))
NN = (((1,), (0,)), ((), ()))
TN = (((0,), (0,)), ((), ()))
BF = jnp.bfloat16
F32 = jnp.float32
GROUP = 16
SLOTS = GROUP * 64
PART = 8


def place():
    grp, tile = lax.axis_index("grp"), lax.axis_index("tile")
    core = tile % 2
    x_hi = (tile // 2) % 2
    y = (tile // 4) % 4
    z = tile // 16
    return grp, z, y, x_hi, core


def dev(grp, z, y, x_hi, core):
    return (grp, ((z * 4 + y) * 2 + x_hi) * 2 + core)


def near_peers(grp, z, y, x_hi, core):
    group = []
    for step in range(1, 8):
        g1, h1, c1 = step // 4, (step // 2) % 2, step % 2
        group.append(((grp + g1) % 2, (x_hi + h1) % 2, (core + c1) % 2))
    return group


def greet(grp, z, y, x_hi, core, others=()):
    barrier = pltpu.get_barrier_semaphore()
    count = 0
    for g1, h1, c1 in near_peers(grp, z, y, x_hi, core):
        pl.semaphore_signal(barrier, inc=1, device_id=dev(g1, z, y, h1, c1), device_id_type=MESH)
        count += 1
    for step in range(1, 8):
        pl.semaphore_signal(
            barrier, inc=1, device_id=dev(grp, (z + step) % 8, y, x_hi, core), device_id_type=MESH
        )
        count += 1
    for step in range(1, 4):
        pl.semaphore_signal(
            barrier, inc=1, device_id=dev(grp, z, (y + step) % 4, x_hi, core), device_id_type=MESH
        )
        count += 1
    for other in others:
        pl.semaphore_signal(barrier, inc=1, device_id=other, device_id_type=MESH)
        count += 1
    pl.semaphore_wait(barrier, count)


def gather_kernel(
    shard_ref, fine_ref, nbr_ref, clinks_ref, near_ref, fnear_ref, extra_ref,
    got, ctx, held, hots, fhots, acc, xacc,
    s1, r1, s2, r2, s3, r3, s4, r4, s5, r5, s6,
):
    grp, z, y, x_hi, core = place()
    tile = lax.axis_index("tile")
    tiles = lax.axis_size("tile")
    right = (grp, (tile + 1) % tiles)
    left = (grp, (tile + tiles - 1) % tiles)
    spot = grp * 4 + x_hi * 2 + core
    pts = fine_ref.shape[1]
    groups = nbr_ref.shape[0] // GROUP
    load = pltpu.make_async_copy(fine_ref, ctx.at[:, pl.ds(RIM, pts)], s6)
    load.start()
    lane = lax.broadcasted_iota(jnp.int32, (32, LANES), 1) % 32
    tiled = jnp.where(lane == lax.broadcasted_iota(jnp.int32, (32, LANES), 0), jnp.float32(1), jnp.float32(0))
    got[spot] = dot(shard_ref[...], tiled.astype(BF), TN).astype(BF)
    greet(grp, z, y, x_hi, core, (left, right))
    first = []
    for k, (g1, h1, c1) in enumerate(near_peers(grp, z, y, x_hi, core)):
        part = got.at[spot, pl.ds(pl.multiple_of(c1 * 32, 32), 32), :]
        copy = pltpu.make_async_remote_copy(
            src_ref=part, dst_ref=part, send_sem=s1.at[k], recv_sem=r1.at[k],
            device_id=dev(g1, z, y, h1, c1), device_id_type=MESH,
        )
        copy.start()
        first.append(copy)
    rim = pltpu.make_async_remote_copy(
        src_ref=fine_ref.at[:, pl.ds(pts - RIM, RIM)], dst_ref=ctx.at[:, pl.ds(0, RIM)],
        send_sem=s5, recv_sem=r5, device_id=right, device_id_type=MESH,
    )
    rim.start()
    flos, los = [], []
    for g in range(groups):
        lo, hi = fine_slots(nbr_ref, g)
        flos.append(lo)
        fhots[g] = one_hot(hi)
    load.wait()

    def pick_own(g):
        found = jnp.zeros((64, SLOTS), F32)
        for part in range(g + 1):
            found = picked(lane_rows(ctx, 4 + part * PART, PART), fhots[g], flos[g], 4 + part * PART, found)
        fnear_ref[g] = found.astype(BF)

    def pick_rim(g):
        found = picked(lane_rows(ctx, 0, 4), fhots[g], flos[g], 0, fnear_ref[g].astype(F32))
        fnear_ref[g] = found.astype(BF)

    pick_own(0)
    pick_own(1)
    for copy in first:
        copy.wait()
    rows = pl.ds(pl.multiple_of(core * 32, 32), 32)
    lane = lax.broadcasted_iota(jnp.int32, (32, LANES), 1) // 32
    for g in range(2):
        chunk = got[g * 4, rows, :].astype(F32)
        for k in range(1, 4):
            chunk = jnp.where(lane == k, got[g * 4 + k, rows, :].astype(F32), chunk)
        held[z, y, core, :, g * LANES : g * LANES + LANES] = chunk.astype(BF)
    along_z, along_y, swap = {}, {}, {}
    for dz in (4, 3, 5, 2, 6, 1, 7):
        part = held.at[z, y, core]
        along_z[dz] = pltpu.make_async_remote_copy(
            src_ref=part, dst_ref=part, send_sem=s2.at[dz - 1], recv_sem=r2.at[dz - 1],
            device_id=dev(grp, (z + dz) % 8, y, x_hi, core), device_id_type=MESH,
        )
        along_z[dz].start()

    def send_y(dz):
        if dz > 0:
            along_z[dz].wait()
        for k in (1, 0, 2):
            part = held.at[(z + 8 - dz) % 8, y, core]
            copy = pltpu.make_async_remote_copy(
                src_ref=part, dst_ref=part, send_sem=s3.at[dz, k], recv_sem=r3.at[dz, k],
                device_id=dev(grp, z, (y + k + 1) % 4, x_hi, core), device_id_type=MESH,
            )
            copy.start()
            along_y[dz, k] = copy

    def send_swap(dz):
        for k in range(3):
            along_y[dz, k].wait()
        part = held.at[(z + 8 - dz) % 8, :, core]
        swap[dz] = pltpu.make_async_remote_copy(
            src_ref=part, dst_ref=part, send_sem=s4.at[dz], recv_sem=r4.at[dz],
            device_id=dev(grp, z, y, x_hi, 1 - core), device_id_type=MESH,
        )
        swap[dz].start()

    def pick_coarse(pair, start, end):
        origins = [(z + 8 - dz) % 8 for dz in pair]
        for dz in pair:
            swap[dz].wait()
        lhs = jnp.concatenate([held[origin].reshape(WIDE, WIDE) for origin in origins], axis=0)

        def choose(hot, lo, found):
            hits = dot(lhs, hot, NN)
            for j, origin in enumerate(origins):
                for yy in range(4):
                    at = (j * 4 + yy) * 64
                    found = jnp.where(lo == origin * 4 + yy, hits[at : at + 64], found)
            return found

        for g in range(groups):
            found = choose(hots[g], los[g], jnp.zeros((64, SLOTS), F32) if start else acc[g])
            if end:
                near_ref[g] = found.astype(BF)
            else:
                acc[g] = found
        found = choose(xhot, xlo, jnp.zeros((64, LANES), F32) if start else xacc[...])
        if end:
            extra_ref[0] = found.astype(BF)
        else:
            xacc[...] = found

    send_y(0)
    for g in range(groups):
        lo, hi = coarse_slots(slots(nbr_ref, g, 0))
        los.append(lo)
        hots[g] = one_hot(hi)
    xlo, xhi = coarse_slots(clinks_ref[pl.ds(grp * (tiles // 4) + tile // 4, 1), :])
    xhot = one_hot(xhi)
    pick_own(2)
    send_y(1)
    send_y(7)
    pick_own(3)
    send_y(2)
    send_y(6)
    send_swap(0)
    for g in range(4, groups):
        pick_own(g)
    send_y(3)
    send_y(5)
    send_swap(1)
    send_swap(7)
    rim.wait()
    for g in range(groups):
        pick_rim(g)
    send_y(4)
    send_swap(2)
    send_swap(6)
    pick_coarse((0, 1), True, False)
    send_swap(3)
    send_swap(5)
    pick_coarse((7, 2), False, False)
    send_swap(4)
    pick_coarse((6, 3), False, False)
    pick_coarse((5, 4), False, True)
    own = held[z, y].reshape(64, WIDE)
    extra_ref[1] = jnp.where(grp == 1, own[:, LANES:].astype(F32), own[:, :LANES].astype(F32)).astype(BF)


def gather_call(coarse_shard, fine_probe, nbr, clinks):
    vmem = pl.BlockSpec(memory_space=pltpu.VMEM)
    dma = pltpu.SemaphoreType.DMA
    groups = nbr.shape[0] // GROUP
    near = jax.ShapeDtypeStruct((groups, 64, SLOTS), BF)
    return pl.pallas_call(
        gather_kernel,
        name="coarse_gather",
        out_shape=(near, near, jax.ShapeDtypeStruct((2, 64, LANES), BF)),
        in_specs=[vmem, pl.BlockSpec(memory_space=pl.ANY), vmem, vmem],
        out_specs=(vmem, vmem, vmem),
        scratch_shapes=[
            pltpu.VMEM((8, 64, LANES), BF),
            pltpu.VMEM((64, RIM + fine_probe.shape[1]), BF),
            pltpu.VMEM((8, 4, 2, 32, WIDE), BF),
            pltpu.VMEM((groups, WIDE, SLOTS), BF),
            pltpu.VMEM((groups, WIDE, SLOTS), BF),
            pltpu.VMEM((groups, 64, SLOTS), F32),
            pltpu.VMEM((64, LANES), F32),
            dma((7,)), dma((7,)), dma((7,)), dma((7,)), dma((8, 3)), dma((8, 3)), dma((8,)), dma((8,)),
            dma, dma, dma,
        ],
        compiler_params=pltpu.CompilerParams(
            collective_id=0, has_side_effects=True, vmem_limit_bytes=60 * 1024 * 1024
        ),
    )(coarse_shard, fine_probe, nbr, clinks)


def sum_kernel(
    terms_ref, fterms_ref, extra_ref, xown_ref, nbr_ref, clinks_ref, own_ref, back_ref, fine_ref, rim_in,
    hots, fhots, totals, rim_out, piece, half_out, half_in, acc, y_out, y_in, z_out, z_in, x_out, x_in,
    s1, r1, s2, r2, s3, r3, s4, r4, s5, r5, s6, s7,
):
    grp, z, y, x_hi, core = place()
    tile = lax.axis_index("tile")
    tiles = lax.axis_size("tile")
    right = (grp, (tile + 1) % tiles)
    left = (grp, (tile + tiles - 1) % tiles)
    mine = pl.ds(pl.multiple_of(core * 32, 32), 32)
    other = pl.ds(pl.multiple_of((1 - core) * 32, 32), 32)
    groups = nbr_ref.shape[0] // GROUP
    load = pltpu.make_async_copy(own_ref, totals, s6)
    load.start()
    los, flos = [], []
    for g in range(groups):
        lo, hi = coarse_slots(slots(nbr_ref, g, 0))
        los.append(lo.astype(BF))
        hots[g] = one_hot(hi)
    xlo, xhi = coarse_slots(clinks_ref[pl.ds(grp * (tiles // 4) + tile // 4, 1), :])
    xlo = xlo.astype(BF)
    xhot = one_hot(xhi)
    swap, along_y, along_z = {}, {}, {}

    def spread_coarse(pair):
        targets = [(z + dz) % 8 for dz in pair]

        def lay(terms, lo):
            zero = jnp.zeros_like(terms)
            return jnp.concatenate(
                [jnp.where(lo == (target * 4 + yy).astype(F32).astype(BF), terms, zero)
                 for target in targets for yy in range(4)],
                axis=0,
            )

        total = dot(lay(extra_ref[...], xlo), xhot, NT)
        for g in range(groups):
            total = total + dot(lay(terms_ref[g], los[g]), hots[g], NT)
        for j, dz in enumerate(pair):
            for yy in range(4):
                at = (j * 4 + yy) * 64
                part = total[at : at + 64]
                if dz == 0:
                    own, none = xown_ref[...], jnp.zeros((64, LANES), F32)
                    here = y == yy
                    part = part + jnp.concatenate(
                        [jnp.where(here & (grp == 0), own, none), jnp.where(here & (grp == 1), own, none)], axis=1
                    )
                piece[dz, yy] = part
                half_out[dz, yy] = piece[dz, yy, other, :].astype(BF)

    def send_swap(dz):
        swap[dz] = pltpu.make_async_remote_copy(
            src_ref=half_out.at[dz], dst_ref=half_in.at[dz], send_sem=s1.at[dz], recv_sem=r1.at[dz],
            device_id=dev(grp, z, y, x_hi, 1 - core), device_id_type=MESH,
        )
        swap[dz].start()

    def send_y(dz):
        swap[dz].wait()
        for yy in range(4):
            total = piece[dz, yy, mine, :] + half_in[dz, yy].astype(F32)
            acc[dz, yy] = total
            y_out[dz, yy] = total.astype(BF)
        for k in (1, 0, 2):
            copy = pltpu.make_async_remote_copy(
                src_ref=y_out.at[dz, (y + k + 1) % 4], dst_ref=y_in.at[dz, k],
                send_sem=s2.at[dz, k], recv_sem=r2.at[dz, k],
                device_id=dev(grp, z, (y + k + 1) % 4, x_hi, core), device_id_type=MESH,
            )
            copy.start()
            along_y[dz, k] = copy

    def send_z(dz):
        total = acc[dz, y]
        for k in range(3):
            along_y[dz, k].wait()
            total = total + y_in[dz, k].astype(F32)
        if dz == 0:
            return total
        z_out[dz - 1] = total.astype(BF)
        along_z[dz] = pltpu.make_async_remote_copy(
            src_ref=z_out.at[dz - 1], dst_ref=z_in.at[dz - 1], send_sem=s3.at[dz - 1], recv_sem=r3.at[dz - 1],
            device_id=dev(grp, (z + dz) % 8, y, x_hi, core), device_id_type=MESH,
        )
        along_z[dz].start()

    def spread_sum(first, parts, start):
        total = None
        for g in range(start, groups):
            found = dot(spread(fterms_ref[g], flos[g], first, parts), fhots[g], NT)
            total = found if total is None else total + found
        return total

    stores = []

    def spread_own(part):
        found = spread_sum(4 + part * PART, PART, part)
        for j in range(PART):
            at = (part * PART + j) * WIDE
            totals[:, at : at + WIDE] = totals[:, at : at + WIDE] + found[j * 64 : j * 64 + 64]
        at = pl.ds(part * PART * WIDE, PART * WIDE)
        store = pltpu.make_async_copy(totals.at[:, at], fine_ref.at[:, at], s7.at[part])
        store.start()
        stores.append(store)

    spread_coarse((4, 3))
    greet(grp, z, y, x_hi, core, (left, right))
    send_swap(4)
    send_swap(3)
    spread_coarse((5, 2))
    send_swap(5)
    send_swap(2)
    send_y(4)
    send_y(3)
    spread_coarse((6, 1))
    send_swap(6)
    send_swap(1)
    send_y(5)
    send_y(2)
    spread_coarse((7, 0))
    send_swap(7)
    send_swap(0)
    send_y(6)
    send_y(1)
    send_z(4)
    send_z(3)
    for g in range(groups):
        lo, hi = fine_slots(nbr_ref, g)
        flos.append(lo.astype(BF))
        fhots[g] = one_hot(hi)
    send_y(7)
    send_y(0)
    send_z(5)
    send_z(2)
    rim_terms = spread_sum(0, 4, 0)
    for j in range(4):
        rim_out[:, j * WIDE : j * WIDE + WIDE] = rim_terms[j * 64 : j * 64 + 64].astype(BF)
    rim = pltpu.make_async_remote_copy(
        src_ref=rim_out, dst_ref=rim_in, send_sem=s5, recv_sem=r5,
        device_id=left, device_id_type=MESH,
    )
    rim.start()
    send_z(6)
    send_z(1)
    load.wait()
    spread_own(0)
    send_z(7)
    total = send_z(0)
    spread_own(1)
    for dz in (4, 3, 5, 2, 6, 1, 7):
        along_z[dz].wait()
        total = total + z_in[dz - 1].astype(F32)
    for g in range(2):
        x_out[g] = total[:, g * LANES : g * LANES + LANES]
    third = []
    spot = grp * 4 + x_hi * 2 + core
    for k, (g1, h1, c1) in enumerate(near_peers(grp, z, y, x_hi, core)):
        copy = pltpu.make_async_remote_copy(
            src_ref=x_out.at[g1], dst_ref=x_in.at[spot], send_sem=s4.at[k], recv_sem=r4.at[k],
            device_id=dev(g1, z, y, h1, c1), device_id_type=MESH,
        )
        copy.start()
        third.append(copy)
    x_in[spot] = x_out[grp]
    for part in range(2, groups):
        spread_own(part)
    rim.wait()
    for copy in third:
        copy.wait()
    which = x_hi * 2 + core
    total = jnp.concatenate(
        [(x_in[half] + x_in[2 + half]) + (x_in[4 + half] + x_in[6 + half]) for half in range(2)], axis=0
    ).T
    part = total[0:32]
    for k in range(1, 4):
        part = jnp.where(which == k, total[k * 32 : k * 32 + 32], part)
    back_ref[...] = part
    for store in stores:
        store.wait()


def sum_call(terms, fterms, xterms, xown, nbr, clinks, own_back):
    vmem = pl.BlockSpec(memory_space=pltpu.VMEM)
    away = pl.BlockSpec(memory_space=pl.ANY)
    dma = pltpu.SemaphoreType.DMA
    groups = nbr.shape[0] // GROUP
    return pl.pallas_call(
        sum_kernel,
        name="coarse_sum",
        out_shape=(
            jax.ShapeDtypeStruct((32, 64), F32),
            jax.ShapeDtypeStruct(own_back.shape, F32),
            jax.ShapeDtypeStruct((64, RIM), BF),
        ),
        in_specs=[vmem] * 6 + [away],
        out_specs=(vmem, away, vmem),
        scratch_shapes=[
            pltpu.VMEM((groups, WIDE, SLOTS), BF),
            pltpu.VMEM((groups, WIDE, SLOTS), BF),
            pltpu.VMEM(own_back.shape, F32),
            pltpu.VMEM((64, RIM), BF),
            pltpu.VMEM((8, 4, 64, WIDE), F32),
            pltpu.VMEM((8, 4, 32, WIDE), BF),
            pltpu.VMEM((8, 4, 32, WIDE), BF),
            pltpu.VMEM((8, 4, 32, WIDE), F32),
            pltpu.VMEM((8, 4, 32, WIDE), BF),
            pltpu.VMEM((8, 3, 32, WIDE), BF),
            pltpu.VMEM((7, 32, WIDE), BF),
            pltpu.VMEM((7, 32, WIDE), BF),
            pltpu.VMEM((2, 32, LANES), F32),
            pltpu.VMEM((8, 32, LANES), F32),
            dma((8,)), dma((8,)), dma((8, 3)), dma((8, 3)), dma((7,)), dma((7,)), dma((7,)), dma((7,)),
            dma, dma, dma, dma((groups,)),
        ],
        compiler_params=pltpu.CompilerParams(
            collective_id=1, has_side_effects=True, vmem_limit_bytes=60 * 1024 * 1024
        ),
    )(terms, fterms, xterms, xown, nbr, clinks, own_back)


def one_hot(hi):
    spots = lax.broadcasted_iota(jnp.int32, (WIDE, hi.shape[1]), 0)
    return jnp.where(spots == hi, jnp.float32(1), jnp.float32(0)).astype(BF)


def dot(a, b, dims):
    return lax.dot_general(a, b, dims, preferred_element_type=F32)


def picked(rows, hot, lo, first, acc):
    found = dot(rows, hot, NN)
    for j in range(found.shape[0] // 64):
        acc = jnp.where(lo == first + j, found[j * 64 : j * 64 + 64], acc)
    return acc


def spread(terms, lo, first, parts):
    zero = jnp.zeros_like(terms)
    return jnp.concatenate([jnp.where(lo == (first + j), terms, zero) for j in range(parts)], axis=0)


def halves(a, b):
    lane = lax.broadcasted_iota(jnp.int32, a.shape, 1)
    low = lane < 64
    return (
        jnp.where(low, a, pltpu.roll(b, 64, 1)),
        jnp.where(low, pltpu.roll(a, 64, 1), b),
    )


def lane_rows(ref, first, parts):
    return jnp.concatenate([ref[:, (first + j) * WIDE : (first + j + 1) * WIDE] for j in range(parts)], axis=0)


def slots(nbr_ref, g, which):
    rows = [nbr_ref[pl.ds(g * GROUP + r, 1), :] for r in range(GROUP)]
    return jnp.concatenate([halves(rows[r], rows[r + 1])[which] for r in range(0, GROUP, 2)], axis=1)


def fine_slots(nbr_ref, g):
    at = slots(nbr_ref, g, 1) - 8192
    return at >> 8, at & 255


def coarse_slots(at):
    lo = jnp.where(at < 0, -1, (at >> 7) & 31)
    return lo, ((at >> 12) << 7) + (at & 127)


def block_kernel(
    near_ref, fnear_ref, extra_ref, fine_ref, diag_ref, cond_ref, cdiag_ref, ccond_ref,
    out_ref, back_ref, cout_ref, terms_ref, fterms_ref, xterms_ref, xown_ref,
):
    g = pl.program_id(0)

    @pl.when(g == 0)
    def _():
        res = dot(cdiag_ref[...], extra_ref[1], NT) + dot(ccond_ref[...], extra_ref[0], NT)
        res = res.astype(BF)
        cout_ref[...] = res
        xown_ref[...] = dot(res, cdiag_ref[...], TN)
        xterms_ref[...] = dot(res, ccond_ref[...], TN).astype(BF)

    nears, results, backs = [], [], []
    for pair in range(GROUP // 2):
        lanes = slice(pair * LANES, pair * LANES + LANES)
        nears.extend(halves(near_ref[:, lanes].astype(F32), fnear_ref[:, lanes].astype(F32)))
    for r in range(GROUP):
        at = r * LANES
        both = jnp.concatenate([diag_ref[at : at + LANES, :], cond_ref[at : at + LANES, :]], axis=1)
        pair = jnp.concatenate([fine_ref[:, at : at + LANES], nears[r].astype(BF)], axis=1)
        results.append(dot(pair, both, NT).astype(BF))
    for r in range(GROUP):
        at = r * LANES
        out_ref[:, at : at + LANES] = results[r]
        both = jnp.concatenate([diag_ref[at : at + LANES, :], cond_ref[at : at + LANES, :]], axis=1)
        back = dot(results[r], both, NN)
        back_ref[:, at : at + LANES] = back[:, :LANES]
        backs.append(back[:, LANES:])
    terms = [halves(backs[r], backs[r + 1]) for r in range(0, GROUP, 2)]
    fterms_ref[...] = jnp.concatenate([pair[1] for pair in terms], axis=1).astype(BF)
    terms_ref[...] = jnp.concatenate([pair[0] for pair in terms], axis=1).astype(BF)


def block_call(near, fnear, extra, fine_probe, diag, cond, cdiag, ccond):
    pts = fine_probe.shape[1]
    steps = near.shape[0]
    whole = lambda *shape: pl.BlockSpec(shape, lambda g: (0,) * len(shape))
    span = GROUP * LANES
    columns = pl.BlockSpec((64, span), lambda g: (0, g))
    slotted = pl.BlockSpec((None, 64, SLOTS), lambda g: (g, 0, 0))
    rows = pl.BlockSpec((span, LANES), lambda g: (g, 0))
    return pl.pallas_call(
        block_kernel,
        name="blocks",
        grid=(steps,),
        out_shape=(
            jax.ShapeDtypeStruct((64, pts), BF),
            jax.ShapeDtypeStruct((64, pts), F32),
            jax.ShapeDtypeStruct((32, 64), BF),
            jax.ShapeDtypeStruct(near.shape, BF),
            jax.ShapeDtypeStruct(near.shape, BF),
            jax.ShapeDtypeStruct((64, LANES), BF),
            jax.ShapeDtypeStruct((64, LANES), F32),
        ),
        in_specs=[
            slotted, slotted, whole(2, 64, LANES), columns, rows, rows, whole(32, LANES), whole(32, LANES),
        ],
        out_specs=(
            columns, columns, whole(32, 64), slotted, slotted, whole(64, LANES), whole(64, LANES),
        ),
        compiler_params=pltpu.CompilerParams(vmem_limit_bytes=60 * 1024 * 1024),
    )(near, fnear, extra, fine_probe, diag, cond, cdiag, ccond)


def on_device(
    fine_probe, coarse_probe, fine_diag, fine_cond, fine_nbr, coarse_diag, coarse_cond, coarse_nbr
):
    near, fine_near, extra = gather_call(coarse_probe.T, fine_probe, fine_nbr, coarse_nbr)
    fine_out, own_back, coarse_out, terms, fine_terms, extra_terms, extra_own = block_call(
        near, fine_near, extra, fine_probe, fine_diag, fine_cond, coarse_diag, coarse_cond
    )
    coarse_back, fine_back, rim_in = sum_call(
        terms, fine_terms, extra_terms, extra_own, fine_nbr, coarse_nbr, own_back
    )
    last = lax.axis_index("tile") == lax.axis_size("tile") - 1
    rim_in = jnp.where(last, jnp.zeros((), F32), rim_in.astype(F32))
    fine_back = fine_back + jnp.pad(rim_in, ((0, 0), (fine_back.shape[1] - RIM, 0)))
    return fine_out, fine_back, coarse_out.T, coarse_back.T


def solution(mesh):
    columns, rows = P(None, ("grp", "tile")), P(("grp", "tile"), None)
    return jax.shard_map(
        on_device,
        mesh=mesh,
        in_specs=(columns, columns, rows, rows, rows, rows, rows, P()),
        out_specs=(columns, columns, columns, columns),
        check_vma=False,
    )
```

time: 84.1 us -> 81.4 us (0.968)
  other arithmetic: 0 us -> 4.37 us
  Pallas kernels: 79.2 us -> 75.4 us
  local copies, waits for them, and re-layouts: 4.04 us -> 0.61 us
    pallas_call x1, Pallas kernels: 20.2 us -> 8.62 us  [block_call(): pl.pallas_call(block_kernel, name='blocks', grid=(steps,), out_shape=(jax...]
    pallas_call x1, Pallas kernels: 26.7 us -> 31.8 us  [sum_call(): pl.pallas_call(sum_kernel, name='coarse_sum', out_shape=(jax.ShapeDtypeSt...]
    add x0 -> x1, other arithmetic: none -> 3.45 us  [on_device(): fine_back + jnp.pad(rim_in, ((0, 0), (fine_back.shape[1] - RIM, 0)))]
    unnamed x4 -> x3, local copies, waits for them, and re-layouts: 4.04 us -> 0.61 us
    pallas_call x1, Pallas kernels: 32.3 us -> 34.9 us  [gather_call(): pl.pallas_call(gather_kernel, name='coarse_gather', out_shape=(near, near...]
    select_n x0 -> x1, other arithmetic: none -> 0.93 us  [on_device(): rim_in = jnp.where(last, jnp.zeros((), F32), rim_in.astype(F32))]
where the time goes in v3:
time: 81.4 us; the launch traced here: 81 us
  Pallas kernels  75.4 us (93%)
  other arithmetic  4.37 us (5%)
    pallas_call x1, Pallas kernels, gather_call(): pl.pallas_call(gather_kernel, name='coarse_gather', out_shape=(near, near...  34.9 us
    pallas_call x1, Pallas kernels, sum_call(): pl.pallas_call(sum_kernel, name='coarse_sum', out_shape=(jax.ShapeDtypeSt...  31.8 us
    pallas_call x1, Pallas kernels, block_call(): pl.pallas_call(block_kernel, name='blocks', grid=(steps,), out_shape=(jax...  8.62 us
    add x1, other arithmetic, on_device(): fine_back + jnp.pad(rim_in, ((0, 0), (fine_back.shape[1] - RIM, 0)))  3.45 us

profile of v3, /device:TPU:1, one launch (start us, length us, event | category | flops | bytes accessed | tf_op | source)
XLA Modules:
  0.0 81.0 jit_solution(4779539862967688208)
XLA Ops:
  0.6 34.9 %coarse_gather.1 = (bf16[5,64,1024]{2,1,0:T(8,128)(2,1)}, bf16[5,64,1024]{2,1,0:T(8,128)(2,1)}, bf16[2,64,128]{2,1,0:T(8,128)(2,1)}) custom-call(bf16[32,64]{1,0:T(8,128)(2,1)} %bitcast.4, bf16[64,10240]{1,0:T(8,128)(2,1)} %fine_ref.3, s32[80,128]{1,0:T(8,128)} %nbr_ref.3, s32[64,128]{1,0:T(8,128)} %clinks_ref.3), custom_call_target="tpu_custom_call" | custom-call | tf_op jit(solution)/shard_map/coarse_gather/pallas_call | solution.py:225
  35.6 8.6 %blocks.1 = (bf16[64,10240]{1,0:T(8,128)(2,1)}, f32[64,10240]{1,0:T(8,128)}, bf16[32,64]{1,0:T(8,128)(2,1)}, bf16[5,64,1024]{2,1,0:T(8,128)(2,1)}, bf16[5,64,102...) custom-call(bf16[5,64,1024]{2,1,0:T(8,128)(2,1)} %get-tuple-element.17.near_ref, ...), custom_call_target="tpu_custom_call" | custom-call | tf_op jit(solution)/shard_map/blocks/pallas_call | solution.py:562
  44.2 31.8 %coarse_sum.1 = (f32[32,64]{1,0:T(8,128)}, f32[64,10240]{1,0:T(8,128)}, bf16[64,1024]{1,0:T(8,128)(2,1)}) custom-call(bf16[5,64,1024]{2,1,0:T(8,128)(2,1)} %get-tuple-element.21.terms_ref, bf16[5,64,1024]{2,1,0:T(8,128)(2,1)} %get-tuple-element.22.fterms_ref, bf16[64,128]{1,0:T(8,128)(2,1)} %get-tuple-element.23.extra_ref, ...), custom_call_target="tpu_custom_call" | custom-call | tf_op jit(solution)/shard_map/coarse_sum/pallas_call | solution.py:436
  76.0 0.9 %convert_select_fusion = f32[64,1024]{1,0:T(8,128)S(1)} fusion(bf16[64,1024]{1,0:T(8,128)(2,1)} %get-tuple-element.27, pred[]{:T(512)S(6)} %eq.3), kind=kLoop, calls=%fused_computation.1 | loop fusion | flops 131072 | bytes 393217 | tf_op jit(solution)/shard_map/jit(_where)/select_n | solution.py:596
  77.0 0.0 copy-start
  77.0 3.4 %pad_add_fusion = f32[64,10240]{1,0:T(8,128)} fusion(f32[64,10240]{1,0:T(8,128)} %get-tuple-element.26, f32[64,1024]{1,0:T(8,128)S(1)} %convert_select_fusion), kind=kLoop, calls=%fused_computation | loop fusion | flops 655360 | bytes 5505024 | tf_op jit(solution)/shard_map/add | solution.py:597
  80.4 0.0 copy-done
  80.4 0.6 copy.13
Async XLA Ops:
  77.0 3.5 %copy-start = (f32[32,64]{1,0:T(8,128)S(1)}, f32[32,64]{1,0:T(8,128)}, u32[]{:S(2)}) copy-start(f32[32,64]{1,0:T(8,128)} %get-tuple-element.29) | copy-start | bytes 24580

commit v4 on v3

--- a/solution.py
+++ b/solution.py
@@ -59,7 +59,7 @@
     for other in others:
         pl.semaphore_signal(barrier, inc=1, device_id=other, device_id_type=MESH)
         count += 1
-    pl.semaphore_wait(barrier, count)
+    return barrier, count
 
 
 def gather_kernel(
@@ -79,8 +79,9 @@
     load.start()
     lane = lax.broadcasted_iota(jnp.int32, (32, LANES), 1) % 32
     tiled = jnp.where(lane == lax.broadcasted_iota(jnp.int32, (32, LANES), 0), jnp.float32(1), jnp.float32(0))
+    barrier, count = greet(grp, z, y, x_hi, core, (left, right))
     got[spot] = dot(shard_ref[...], tiled.astype(BF), TN).astype(BF)
-    greet(grp, z, y, x_hi, core, (left, right))
+    pl.semaphore_wait(barrier, count)
     first = []
     for k, (g1, h1, c1) in enumerate(near_peers(grp, z, y, x_hi, core)):
         part = got.at[spot, pl.ds(pl.multiple_of(c1 * 32, 32), 32), :]
@@ -94,7 +95,6 @@
         src_ref=fine_ref.at[:, pl.ds(pts - RIM, RIM)], dst_ref=ctx.at[:, pl.ds(0, RIM)],
         send_sem=s5, recv_sem=r5, device_id=right, device_id_type=MESH,
     )
-    rim.start()
     flos, los = [], []
     for g in range(groups):
         lo, hi = fine_slots(nbr_ref, g)
@@ -124,7 +124,7 @@
             chunk = jnp.where(lane == k, got[g * 4 + k, rows, :].astype(F32), chunk)
         held[z, y, core, :, g * LANES : g * LANES + LANES] = chunk.astype(BF)
     along_z, along_y, swap = {}, {}, {}
-    for dz in (4, 3, 5, 2, 6, 1, 7):
+    for dz in (1, 7, 2, 6, 3, 5, 4):
         part = held.at[z, y, core]
         along_z[dz] = pltpu.make_async_remote_copy(
             src_ref=part, dst_ref=part, send_sem=s2.at[dz - 1], recv_sem=r2.at[dz - 1],
@@ -181,36 +181,37 @@
             xacc[...] = found
 
     send_y(0)
+    rim.start()
     for g in range(groups):
         lo, hi = coarse_slots(slots(nbr_ref, g, 0))
         los.append(lo)
         hots[g] = one_hot(hi)
     xlo, xhi = coarse_slots(clinks_ref[pl.ds(grp * (tiles // 4) + tile // 4, 1), :])
     xhot = one_hot(xhi)
-    pick_own(2)
     send_y(1)
     send_y(7)
-    pick_own(3)
+    pick_own(2)
     send_y(2)
     send_y(6)
+    pick_own(3)
+    send_y(3)
+    send_y(5)
+    send_y(4)
     send_swap(0)
     for g in range(4, groups):
         pick_own(g)
-    send_y(3)
-    send_y(5)
     send_swap(1)
     send_swap(7)
     rim.wait()
     for g in range(groups):
         pick_rim(g)
-    send_y(4)
     send_swap(2)
     send_swap(6)
     pick_coarse((0, 1), True, False)
     send_swap(3)
     send_swap(5)
+    send_swap(4)
     pick_coarse((7, 2), False, False)
-    send_swap(4)
     pick_coarse((6, 3), False, False)
     pick_coarse((5, 4), False, True)
     own = held[z, y].reshape(64, WIDE)
@@ -260,6 +261,7 @@
     groups = nbr_ref.shape[0] // GROUP
     load = pltpu.make_async_copy(own_ref, totals, s6)
     load.start()
+    barrier, count = greet(grp, z, y, x_hi, core, (left, right))
     los, flos = [], []
     for g in range(groups):
         lo, hi = coarse_slots(slots(nbr_ref, g, 0))
@@ -353,7 +355,7 @@
         stores.append(store)
 
     spread_coarse((4, 3))
-    greet(grp, z, y, x_hi, core, (left, right))
+    pl.semaphore_wait(barrier, count)
     send_swap(4)
     send_swap(3)
     spread_coarse((5, 2))
@@ -392,9 +394,9 @@
     send_z(6)
     send_z(1)
     load.wait()
-    spread_own(0)
     send_z(7)
     total = send_z(0)
+    spread_own(0)
     spread_own(1)
     for dz in (4, 3, 5, 2, 6, 1, 7):
         along_z[dz].wait()
@@ -582,6 +584,30 @@
     )(near, fnear, extra, fine_probe, diag, cond, cdiag, ccond)
 
 
+def finish_kernel(fine_ref, rim_ref, out_ref):
+    g = pl.program_id(0)
+    out_ref[...] = fine_ref[...]
+
+    @pl.when(g == pl.num_programs(0) - 1)
+    def _():
+        last = lax.axis_index("tile") == lax.axis_size("tile") - 1
+        keep = jnp.where(last, jnp.float32(0), jnp.float32(1))
+        out_ref[:, -RIM:] = fine_ref[:, -RIM:] + rim_ref[...].astype(F32) * keep
+
+
+def finish_call(fine_back, rim):
+    columns = pl.BlockSpec((64, GROUP * LANES), lambda g: (0, g))
+    return pl.pallas_call(
+        finish_kernel,
+        name="add_rim",
+        grid=(fine_back.shape[1] // (GROUP * LANES),),
+        out_shape=jax.ShapeDtypeStruct(fine_back.shape, F32),
+        in_specs=[columns, pl.BlockSpec((64, RIM), lambda g: (0, 0))],
+        out_specs=columns,
+        compiler_params=pltpu.CompilerParams(vmem_limit_bytes=60 * 1024 * 1024),
+    )(fine_back, rim)
+
+
 def on_device(
     fine_probe, coarse_probe, fine_diag, fine_cond, fine_nbr, coarse_diag, coarse_cond, coarse_nbr
 ):
@@ -592,9 +618,7 @@
     coarse_back, fine_back, rim_in = sum_call(
         terms, fine_terms, extra_terms, extra_own, fine_nbr, coarse_nbr, own_back
     )
-    last = lax.axis_index("tile") == lax.axis_size("tile") - 1
-    rim_in = jnp.where(last, jnp.zeros((), F32), rim_in.astype(F32))
-    fine_back = fine_back + jnp.pad(rim_in, ((0, 0), (fine_back.shape[1] - RIM, 0)))
+    fine_back = finish_call(fine_back, rim_in)
     return fine_out, fine_back, coarse_out.T, coarse_back.T
 
 

time: 81.4 us -> 76.4 us (0.939)
  other arithmetic: 4.37 us -> 0 us
    pallas_call x0 -> x1, Pallas kernels: none -> 4.75 us  [finish_call(): pl.pallas_call(finish_kernel, name='add_rim', grid=(fine_back.shape[1] //...]
    pallas_call x1, Pallas kernels: 31.8 us -> 27.4 us  [sum_call(): pl.pallas_call(sum_kernel, name='coarse_sum', out_shape=(jax.ShapeDtypeSt...]
    add x1 -> x0, other arithmetic: 3.45 us -> none  [on_device(): fine_back + jnp.pad(rim_in, ((0, 0), (fine_back.shape[1] - RIM, 0)))]
    pallas_call x1, Pallas kernels: 34.9 us -> 34 us  [gather_call(): pl.pallas_call(gather_kernel, name='coarse_gather', out_shape=(near, near...]
    select_n x1 -> x0, other arithmetic: 0.93 us -> none  [on_device(): rim_in = jnp.where(last, jnp.zeros((), F32), rim_in.astype(F32))]
where the time goes in v4:
time: 76.4 us; the launch traced here: 76 us
  Pallas kernels  74.8 us (98%)
    pallas_call x1, Pallas kernels, gather_call(): pl.pallas_call(gather_kernel, name='coarse_gather', out_shape=(near, near...  34 us
    pallas_call x1, Pallas kernels, sum_call(): pl.pallas_call(sum_kernel, name='coarse_sum', out_shape=(jax.ShapeDtypeSt...  27.4 us
    pallas_call x1, Pallas kernels, block_call(): pl.pallas_call(block_kernel, name='blocks', grid=(steps,), out_shape=(jax...  8.62 us
    pallas_call x1, Pallas kernels, finish_call(): pl.pallas_call(finish_kernel, name='add_rim', grid=(fine_back.shape[1] //...  4.75 us

profile of v4, /device:TPU:1, one launch (start us, length us, event | category | flops | bytes accessed | tf_op | source)
XLA Modules:
  0.0 76.0 jit_solution(434676038123484001)
XLA Ops:
  0.6 34.0 %coarse_gather.1 = (bf16[5,64,1024]{2,1,0:T(8,128)(2,1)}, bf16[5,64,1024]{2,1,0:T(8,128)(2,1)}, bf16[2,64,128]{2,1,0:T(8,128)(2,1)}) custom-call(bf16[32,64]{1,0:T(8,128)(2,1)} %bitcast.4, bf16[64,10240]{1,0:T(8,128)(2,1)} %fine_ref.3, s32[80,128]{1,0:T(8,128)} %nbr_ref.3, s32[64,128]{1,0:T(8,128)} %clinks_ref.3), custom_call_target="tpu_custom_call" | custom-call | tf_op jit(solution)/shard_map/coarse_gather/pallas_call | solution.py:226
  34.6 8.6 %blocks.1 = (bf16[64,10240]{1,0:T(8,128)(2,1)}, f32[64,10240]{1,0:T(8,128)}, bf16[32,64]{1,0:T(8,128)(2,1)}, bf16[5,64,1024]{2,1,0:T(8,128)(2,1)}, bf16[5,64,102...) custom-call(bf16[5,64,1024]{2,1,0:T(8,128)(2,1)} %get-tuple-element.17.near_ref, ...), custom_call_target="tpu_custom_call" | custom-call | tf_op jit(solution)/shard_map/blocks/pallas_call | solution.py:564
  43.2 27.4 %coarse_sum.1 = (f32[32,64]{1,0:T(8,128)}, f32[64,10240]{1,0:T(8,128)}, bf16[64,1024]{1,0:T(8,128)(2,1)}) custom-call(bf16[5,64,1024]{2,1,0:T(8,128)(2,1)} %get-tuple-element.21.terms_ref, bf16[5,64,1024]{2,1,0:T(8,128)(2,1)} %get-tuple-element.22.fterms_ref, bf16[64,128]{1,0:T(8,128)(2,1)} %get-tuple-element.23.extra_ref, ...), custom_call_target="tpu_custom_call" | custom-call | tf_op jit(solution)/shard_map/coarse_sum/pallas_call | solution.py:438
  70.7 0.0 copy-start
  70.7 4.8 %add_rim.1 = f32[64,10240]{1,0:T(8,128)} custom-call(f32[64,10240]{1,0:T(8,128)} %get-tuple-element.26.fine_ref, bf16[64,1024]{1,0:T(8,128)(2,1)} %get-tuple-element.27.rim_ref), custom_call_target="tpu_custom_call" | custom-call | tf_op jit(solution)/shard_map/add_rim/pallas_call | solution.py:600
  75.4 0.0 copy-done
  75.4 0.6 copy.13
Async XLA Ops:
  70.7 4.8 %copy-start = (f32[32,64]{1,0:T(8,128)S(1)}, f32[32,64]{1,0:T(8,128)}, u32[]{:S(2)}) copy-start(f32[32,64]{1,0:T(8,128)} %get-tuple-element.29) | copy-start | bytes 24580

commit v5 on v4

--- a/solution.py
+++ b/solution.py
@@ -247,9 +247,9 @@
 
 
 def sum_kernel(
-    terms_ref, fterms_ref, extra_ref, xown_ref, nbr_ref, clinks_ref, own_ref, back_ref, fine_ref, rim_in,
-    hots, fhots, totals, rim_out, piece, half_out, half_in, acc, y_out, y_in, z_out, z_in, x_out, x_in,
-    s1, r1, s2, r2, s3, r3, s4, r4, s5, r5, s6, s7,
+    terms_ref, extra_ref, xown_ref, nbr_ref, clinks_ref, rim_out, back_ref, rim_in,
+    hots, piece, half_out, half_in, acc, y_out, y_in, z_out, z_in, x_out, x_in,
+    s1, r1, s2, r2, s3, r3, s4, r4, s5, r5,
 ):
     grp, z, y, x_hi, core = place()
     tile = lax.axis_index("tile")
@@ -259,10 +259,8 @@
     mine = pl.ds(pl.multiple_of(core * 32, 32), 32)
     other = pl.ds(pl.multiple_of((1 - core) * 32, 32), 32)
     groups = nbr_ref.shape[0] // GROUP
-    load = pltpu.make_async_copy(own_ref, totals, s6)
-    load.start()
     barrier, count = greet(grp, z, y, x_hi, core, (left, right))
-    los, flos = [], []
+    los = []
     for g in range(groups):
         lo, hi = coarse_slots(slots(nbr_ref, g, 0))
         los.append(lo.astype(BF))
@@ -335,27 +333,12 @@
         )
         along_z[dz].start()
 
-    def spread_sum(first, parts, start):
-        total = None
-        for g in range(start, groups):
-            found = dot(spread(fterms_ref[g], flos[g], first, parts), fhots[g], NT)
-            total = found if total is None else total + found
-        return total
-
-    stores = []
-
-    def spread_own(part):
-        found = spread_sum(4 + part * PART, PART, part)
-        for j in range(PART):
-            at = (part * PART + j) * WIDE
-            totals[:, at : at + WIDE] = totals[:, at : at + WIDE] + found[j * 64 : j * 64 + 64]
-        at = pl.ds(part * PART * WIDE, PART * WIDE)
-        store = pltpu.make_async_copy(totals.at[:, at], fine_ref.at[:, at], s7.at[part])
-        store.start()
-        stores.append(store)
-
     spread_coarse((4, 3))
     pl.semaphore_wait(barrier, count)
+    rim = pltpu.make_async_remote_copy(
+        src_ref=rim_out, dst_ref=rim_in, send_sem=s5, recv_sem=r5,
+        device_id=left, device_id_type=MESH,
+    )
     send_swap(4)
     send_swap(3)
     spread_coarse((5, 2))
@@ -375,29 +358,15 @@
     send_y(1)
     send_z(4)
     send_z(3)
-    for g in range(groups):
-        lo, hi = fine_slots(nbr_ref, g)
-        flos.append(lo.astype(BF))
-        fhots[g] = one_hot(hi)
+    rim.start()
     send_y(7)
     send_y(0)
     send_z(5)
     send_z(2)
-    rim_terms = spread_sum(0, 4, 0)
-    for j in range(4):
-        rim_out[:, j * WIDE : j * WIDE + WIDE] = rim_terms[j * 64 : j * 64 + 64].astype(BF)
-    rim = pltpu.make_async_remote_copy(
-        src_ref=rim_out, dst_ref=rim_in, send_sem=s5, recv_sem=r5,
-        device_id=left, device_id_type=MESH,
-    )
-    rim.start()
     send_z(6)
     send_z(1)
-    load.wait()
     send_z(7)
     total = send_z(0)
-    spread_own(0)
-    spread_own(1)
     for dz in (4, 3, 5, 2, 6, 1, 7):
         along_z[dz].wait()
         total = total + z_in[dz - 1].astype(F32)
@@ -413,8 +382,6 @@
         copy.start()
         third.append(copy)
     x_in[spot] = x_out[grp]
-    for part in range(2, groups):
-        spread_own(part)
     rim.wait()
     for copy in third:
         copy.wait()
@@ -426,13 +393,10 @@
     for k in range(1, 4):
         part = jnp.where(which == k, total[k * 32 : k * 32 + 32], part)
     back_ref[...] = part
-    for store in stores:
-        store.wait()
-
-
-def sum_call(terms, fterms, xterms, xown, nbr, clinks, own_back):
+
+
+def sum_call(terms, xterms, xown, nbr, clinks, rim_terms):
     vmem = pl.BlockSpec(memory_space=pltpu.VMEM)
-    away = pl.BlockSpec(memory_space=pl.ANY)
     dma = pltpu.SemaphoreType.DMA
     groups = nbr.shape[0] // GROUP
     return pl.pallas_call(
@@ -440,16 +404,12 @@
         name="coarse_sum",
         out_shape=(
             jax.ShapeDtypeStruct((32, 64), F32),
-            jax.ShapeDtypeStruct(own_back.shape, F32),
             jax.ShapeDtypeStruct((64, RIM), BF),
         ),
-        in_specs=[vmem] * 6 + [away],
-        out_specs=(vmem, away, vmem),
+        in_specs=[vmem] * 6,
+        out_specs=(vmem, vmem),
         scratch_shapes=[
             pltpu.VMEM((groups, WIDE, SLOTS), BF),
-            pltpu.VMEM((groups, WIDE, SLOTS), BF),
-            pltpu.VMEM(own_back.shape, F32),
-            pltpu.VMEM((64, RIM), BF),
             pltpu.VMEM((8, 4, 64, WIDE), F32),
             pltpu.VMEM((8, 4, 32, WIDE), BF),
             pltpu.VMEM((8, 4, 32, WIDE), BF),
@@ -461,12 +421,12 @@
             pltpu.VMEM((2, 32, LANES), F32),
             pltpu.VMEM((8, 32, LANES), F32),
             dma((8,)), dma((8,)), dma((8, 3)), dma((8, 3)), dma((7,)), dma((7,)), dma((7,)), dma((7,)),
-            dma, dma, dma, dma((groups,)),
+            dma, dma,
         ],
         compiler_params=pltpu.CompilerParams(
             collective_id=1, has_side_effects=True, vmem_limit_bytes=60 * 1024 * 1024
         ),
-    )(terms, fterms, xterms, xown, nbr, clinks, own_back)
+    )(terms, xterms, xown, nbr, clinks, rim_terms)
 
 
 def one_hot(hi):
@@ -519,20 +479,25 @@
 
 
 def block_kernel(
-    near_ref, fnear_ref, extra_ref, fine_ref, diag_ref, cond_ref, cdiag_ref, ccond_ref,
-    out_ref, back_ref, cout_ref, terms_ref, fterms_ref, xterms_ref, xown_ref,
+    near_ref, fnear_ref, extra_ref, fine_ref, nbr_ref, diag_ref, cond_ref, cdiag_ref, ccond_ref,
+    out_ref, back_ref, cout_ref, terms_ref, xterms_ref, xown_ref, rim_ref,
+    totals,
 ):
-    g = pl.program_id(0)
-
-    @pl.when(g == 0)
+    steps = pl.num_programs(0)
+    g = steps - 1 - pl.program_id(0)
+
+    @pl.when(g == steps - 1)
     def _():
+        totals[...] = jnp.zeros_like(totals)
         res = dot(cdiag_ref[...], extra_ref[1], NT) + dot(ccond_ref[...], extra_ref[0], NT)
         res = res.astype(BF)
         cout_ref[...] = res
         xown_ref[...] = dot(res, cdiag_ref[...], TN)
         xterms_ref[...] = dot(res, ccond_ref[...], TN).astype(BF)
 
-    nears, results, backs = [], [], []
+    lo, hi = fine_slots(nbr_ref, g)
+    lo, hot = lo.astype(BF), one_hot(hi)
+    nears, results, backs, own_back = [], [], [], []
     for pair in range(GROUP // 2):
         lanes = slice(pair * LANES, pair * LANES + LANES)
         nears.extend(halves(near_ref[:, lanes].astype(F32), fnear_ref[:, lanes].astype(F32)))
@@ -546,21 +511,42 @@
         out_ref[:, at : at + LANES] = results[r]
         both = jnp.concatenate([diag_ref[at : at + LANES, :], cond_ref[at : at + LANES, :]], axis=1)
         back = dot(results[r], both, NN)
-        back_ref[:, at : at + LANES] = back[:, :LANES]
+        own_back.append(back[:, :LANES])
         backs.append(back[:, LANES:])
     terms = [halves(backs[r], backs[r + 1]) for r in range(0, GROUP, 2)]
-    fterms_ref[...] = jnp.concatenate([pair[1] for pair in terms], axis=1).astype(BF)
     terms_ref[...] = jnp.concatenate([pair[0] for pair in terms], axis=1).astype(BF)
-
-
-def block_call(near, fnear, extra, fine_probe, diag, cond, cdiag, ccond):
+    fterms = jnp.concatenate([pair[1] for pair in terms], axis=1).astype(BF)
+
+    def add(first, parts):
+        found = dot(spread(fterms, lo, first, parts), hot, NT)
+        for j in range(parts):
+            at = slice((first + j) * WIDE, (first + j + 1) * WIDE)
+            totals[:, at] = totals[:, at] + found[j * 64 : j * 64 + 64]
+
+    add(0, 4)
+    for section in range((totals.shape[1] - RIM) // (PART * WIDE)):
+
+        @pl.when(section <= g)
+        def _():
+            add(4 + section * PART, PART)
+
+    span = PART * WIDE
+    mine = pl.ds(pl.multiple_of(RIM + g * span, RIM), span)
+    back_ref[...] = totals[:, mine] + jnp.concatenate(own_back, axis=1)
+
+    @pl.when(g == 0)
+    def _():
+        rim_ref[...] = totals[:, 0:RIM].astype(BF)
+
+
+def block_call(near, fnear, extra, fine_probe, nbr, diag, cond, cdiag, ccond):
     pts = fine_probe.shape[1]
     steps = near.shape[0]
     whole = lambda *shape: pl.BlockSpec(shape, lambda g: (0,) * len(shape))
     span = GROUP * LANES
-    columns = pl.BlockSpec((64, span), lambda g: (0, g))
-    slotted = pl.BlockSpec((None, 64, SLOTS), lambda g: (g, 0, 0))
-    rows = pl.BlockSpec((span, LANES), lambda g: (g, 0))
+    columns = pl.BlockSpec((64, span), lambda g: (0, steps - 1 - g))
+    slotted = pl.BlockSpec((None, 64, SLOTS), lambda g: (steps - 1 - g, 0, 0))
+    rows = pl.BlockSpec((span, LANES), lambda g: (steps - 1 - g, 0))
     return pl.pallas_call(
         block_kernel,
         name="blocks",
@@ -570,40 +556,39 @@
             jax.ShapeDtypeStruct((64, pts), F32),
             jax.ShapeDtypeStruct((32, 64), BF),
             jax.ShapeDtypeStruct(near.shape, BF),
-            jax.ShapeDtypeStruct(near.shape, BF),
             jax.ShapeDtypeStruct((64, LANES), BF),
             jax.ShapeDtypeStruct((64, LANES), F32),
+            jax.ShapeDtypeStruct((64, RIM), BF),
         ),
         in_specs=[
-            slotted, slotted, whole(2, 64, LANES), columns, rows, rows, whole(32, LANES), whole(32, LANES),
+            slotted, slotted, whole(2, 64, LANES), columns, whole(*nbr.shape), rows, rows,
+            whole(32, LANES), whole(32, LANES),
         ],
         out_specs=(
-            columns, columns, whole(32, 64), slotted, slotted, whole(64, LANES), whole(64, LANES),
+            columns, columns, whole(32, 64), slotted, whole(64, LANES), whole(64, LANES), whole(64, RIM),
         ),
+        scratch_shapes=[pltpu.VMEM((64, RIM + pts), F32)],
         compiler_params=pltpu.CompilerParams(vmem_limit_bytes=60 * 1024 * 1024),
-    )(near, fnear, extra, fine_probe, diag, cond, cdiag, ccond)
+    )(near, fnear, extra, fine_probe, nbr, diag, cond, cdiag, ccond)
 
 
 def finish_kernel(fine_ref, rim_ref, out_ref):
-    g = pl.program_id(0)
-    out_ref[...] = fine_ref[...]
-
-    @pl.when(g == pl.num_programs(0) - 1)
-    def _():
-        last = lax.axis_index("tile") == lax.axis_size("tile") - 1
-        keep = jnp.where(last, jnp.float32(0), jnp.float32(1))
-        out_ref[:, -RIM:] = fine_ref[:, -RIM:] + rim_ref[...].astype(F32) * keep
+    last = lax.axis_index("tile") == lax.axis_size("tile") - 1
+    keep = jnp.where(last, jnp.float32(0), jnp.float32(1))
+    out_ref[...] = fine_ref[...] + rim_ref[...].astype(F32) * keep
 
 
 def finish_call(fine_back, rim):
-    columns = pl.BlockSpec((64, GROUP * LANES), lambda g: (0, g))
+    final = fine_back.shape[1] // RIM - 1
+    columns = pl.BlockSpec((64, RIM), lambda g: (0, final))
     return pl.pallas_call(
         finish_kernel,
         name="add_rim",
-        grid=(fine_back.shape[1] // (GROUP * LANES),),
+        grid=(1,),
         out_shape=jax.ShapeDtypeStruct(fine_back.shape, F32),
         in_specs=[columns, pl.BlockSpec((64, RIM), lambda g: (0, 0))],
         out_specs=columns,
+        input_output_aliases={0: 0},
         compiler_params=pltpu.CompilerParams(vmem_limit_bytes=60 * 1024 * 1024),
     )(fine_back, rim)
 
@@ -612,12 +597,10 @@
     fine_probe, coarse_probe, fine_diag, fine_cond, fine_nbr, coarse_diag, coarse_cond, coarse_nbr
 ):
     near, fine_near, extra = gather_call(coarse_probe.T, fine_probe, fine_nbr, coarse_nbr)
-    fine_out, own_back, coarse_out, terms, fine_terms, extra_terms, extra_own = block_call(
-        near, fine_near, extra, fine_probe, fine_diag, fine_cond, coarse_diag, coarse_cond
+    fine_out, fine_back, coarse_out, terms, extra_terms, extra_own, rim_terms = block_call(
+        near, fine_near, extra, fine_probe, fine_nbr, fine_diag, fine_cond, coarse_diag, coarse_cond
     )
-    coarse_back, fine_back, rim_in = sum_call(
-        terms, fine_terms, extra_terms, extra_own, fine_nbr, coarse_nbr, own_back
-    )
+    coarse_back, rim_in = sum_call(terms, extra_terms, extra_own, fine_nbr, coarse_nbr, rim_terms)
     fine_back = finish_call(fine_back, rim_in)
     return fine_out, fine_back, coarse_out.T, coarse_back.T
 

time: 76.4 us -> 78.8 us (1.031)
  Pallas kernels: 74.8 us -> 77.4 us
    pallas_call x1, Pallas kernels: 8.62 us -> 15.4 us  [block_call(): pl.pallas_call(block_kernel, name='blocks', grid=(steps,), out_shape=(jax...]
    pallas_call x1, Pallas kernels: 4.75 us -> 1.72 us  [finish_call(): pl.pallas_call(finish_kernel, name='add_rim', grid=(1,), out_shape=jax.Sh...]
    pallas_call x1, Pallas kernels: 27.4 us -> 26.3 us  [sum_call(): pl.pallas_call(sum_kernel, name='coarse_sum', out_shape=(jax.ShapeDtypeSt...]
where the time goes in v5:
time: 78.8 us; the launch traced here: 78.7 us
  Pallas kernels  77.4 us (98%)
    pallas_call x1, Pallas kernels, gather_call(): pl.pallas_call(gather_kernel, name='coarse_gather', out_shape=(near, near...  34 us
    pallas_call x1, Pallas kernels, sum_call(): pl.pallas_call(sum_kernel, name='coarse_sum', out_shape=(jax.ShapeDtypeSt...  26.3 us
    pallas_call x1, Pallas kernels, block_call(): pl.pallas_call(block_kernel, name='blocks', grid=(steps,), out_shape=(jax...  15.4 us
    pallas_call x1, Pallas kernels, finish_call(): pl.pallas_call(finish_kernel, name='add_rim', grid=(1,), out_shape=jax.Sh...  1.72 us

profile of v5, /device:TPU:1, one launch (start us, length us, event | category | flops | bytes accessed | tf_op | source)
XLA Modules:
  0.0 78.7 jit_solution(14918191034715226957)
XLA Ops:
  0.6 34.0 %coarse_gather.1 = (bf16[5,64,1024]{2,1,0:T(8,128)(2,1)}, bf16[5,64,1024]{2,1,0:T(8,128)(2,1)}, bf16[2,64,128]{2,1,0:T(8,128)(2,1)}) custom-call(bf16[32,64]{1,0:T(8,128)(2,1)} %bitcast.4, bf16[64,10240]{1,0:T(8,128)(2,1)} %fine_ref.3, s32[80,128]{1,0:T(8,128)} %nbr_ref.5, s32[64,128]{1,0:T(8,128)} %clinks_ref.3), custom_call_target="tpu_custom_call" | custom-call | tf_op jit(solution)/shard_map/coarse_gather/pallas_call | solution.py:226
  34.6 15.4 %blocks.1 = (bf16[64,10240]{1,0:T(8,128)(2,1)}, f32[64,10240]{1,0:T(8,128)}, bf16[32,64]{1,0:T(8,128)(2,1)}, bf16[5,64,1024]{2,1,0:T(8,128)(2,1)}, bf16[64,128]{...) custom-call(bf16[5,64,1024]{2,1,0:T(8,128)(2,1)} %get-tuple-element.16.near_ref, ...), custom_call_target="tpu_custom_call" | custom-call | tf_op jit(solution)/shard_map/blocks/pallas_call | solution.py:550
  50.0 26.3 %coarse_sum.1 = (f32[32,64]{1,0:T(8,128)}, bf16[64,1024]{1,0:T(8,128)(2,1)}) custom-call(bf16[5,64,1024]{2,1,0:T(8,128)(2,1)} %get-tuple-element.21.terms_ref, bf16[64,128]{1,0:T(8,128)(2,1)} %get-tuple-element.22.extra_ref, f32[64,128]{1,0:T(8,128)} %get-tuple-element.23.xown_ref, s32[80,128]{1,0:T(8,128)} %nbr_ref.5, s32[64,128]{1,0:T(8,128)} %clinks_ref.3, ...), custom_call_target="tpu_custom_call" | custom-call | tf_op jit(solution)/shard_map/coarse_sum/pallas_call | solution.py:402
  76.3 0.0 copy-start
  76.3 1.7 %add_rim.1 = f32[64,10240]{1,0:T(8,128)} custom-call(f32[64,10240]{1,0:T(8,128)} %get-tuple-element.20.fine_ref, bf16[64,1024]{1,0:T(8,128)(2,1)} %get-tuple-element.25.rim_ref), custom_call_target="tpu_custom_call", output_to_operand_aliasing={{}: (0, {})} | custom-call | tf_op jit(solution)/shard_map/add_rim/pallas_call | solution.py:584
  78.0 0.0 copy-done
  78.0 0.6 copy.15
Async XLA Ops:
  76.3 1.7 %copy-start = (f32[32,64]{1,0:T(8,128)S(1)}, f32[32,64]{1,0:T(8,128)}, u32[]{:S(2)}) copy-start(f32[32,64]{1,0:T(8,128)} %get-tuple-element.27) | copy-start | bytes 24580

commit v6 on v4

--- a/solution.py
+++ b/solution.py
@@ -584,26 +584,39 @@
     )(near, fnear, extra, fine_probe, diag, cond, cdiag, ccond)
 
 
-def finish_kernel(fine_ref, rim_ref, out_ref):
-    g = pl.program_id(0)
-    out_ref[...] = fine_ref[...]
-
-    @pl.when(g == pl.num_programs(0) - 1)
-    def _():
-        last = lax.axis_index("tile") == lax.axis_size("tile") - 1
-        keep = jnp.where(last, jnp.float32(0), jnp.float32(1))
-        out_ref[:, -RIM:] = fine_ref[:, -RIM:] + rim_ref[...].astype(F32) * keep
+def finish_kernel(fine_ref, rim_ref, out_ref, held, into, back):
+    pts = fine_ref.shape[1]
+    pieces = 10
+    span = (pts - RIM) // (pieces - 1)
+    spans = [pl.ds(k * span, span) for k in range(pieces - 1)] + [pl.ds(pts - RIM, RIM)]
+    loads, stores = [], []
+    for k, at in enumerate(spans):
+        load = pltpu.make_async_copy(fine_ref.at[:, at], held.at[:, at], into.at[k])
+        load.start()
+        loads.append(load)
+    for k, at in enumerate(spans):
+        loads[k].wait()
+        if k == pieces - 1:
+            last = lax.axis_index("tile") == lax.axis_size("tile") - 1
+            keep = jnp.where(last, jnp.float32(0), jnp.float32(1))
+            held[:, pts - RIM :] = held[:, pts - RIM :] + rim_ref[...].astype(F32) * keep
+        store = pltpu.make_async_copy(held.at[:, at], out_ref.at[:, at], back.at[k])
+        store.start()
+        stores.append(store)
+    for store in stores:
+        store.wait()
 
 
 def finish_call(fine_back, rim):
-    columns = pl.BlockSpec((64, GROUP * LANES), lambda g: (0, g))
+    away = pl.BlockSpec(memory_space=pl.ANY)
+    dma = pltpu.SemaphoreType.DMA
     return pl.pallas_call(
         finish_kernel,
         name="add_rim",
-        grid=(fine_back.shape[1] // (GROUP * LANES),),
         out_shape=jax.ShapeDtypeStruct(fine_back.shape, F32),
-        in_specs=[columns, pl.BlockSpec((64, RIM), lambda g: (0, 0))],
-        out_specs=columns,
+        in_specs=[away, pl.BlockSpec(memory_space=pltpu.VMEM)],
+        out_specs=away,
+        scratch_shapes=[pltpu.VMEM(fine_back.shape, F32), dma((10,)), dma((10,))],
         compiler_params=pltpu.CompilerParams(vmem_limit_bytes=60 * 1024 * 1024),
     )(fine_back, rim)
 

time: 76.4 us -> 75.2 us (0.984)
  Pallas kernels: 74.8 us -> 73.5 us
    pallas_call x1, Pallas kernels: 4.75 us -> 3.51 us  [finish_call(): pl.pallas_call(finish_kernel, name='add_rim', out_shape=jax.ShapeDtypeStr...]
where the time goes in v6:
time: 75.2 us; the launch traced here: 74.8 us
  Pallas kernels  73.5 us (98%)
    pallas_call x1, Pallas kernels, gather_call(): pl.pallas_call(gather_kernel, name='coarse_gather', out_shape=(near, near...  34 us
    pallas_call x1, Pallas kernels, sum_call(): pl.pallas_call(sum_kernel, name='coarse_sum', out_shape=(jax.ShapeDtypeSt...  27.4 us
    pallas_call x1, Pallas kernels, block_call(): pl.pallas_call(block_kernel, name='blocks', grid=(steps,), out_shape=(jax...  8.62 us
    pallas_call x1, Pallas kernels, finish_call(): pl.pallas_call(finish_kernel, name='add_rim', out_shape=jax.ShapeDtypeStr...  3.51 us

profile of v6, /device:TPU:1, one launch (start us, length us, event | category | flops | bytes accessed | tf_op | source)
XLA Modules:
  0.0 74.8 jit_solution(11404524724967833483)
XLA Ops:
  0.6 34.0 %coarse_gather.1 = (bf16[5,64,1024]{2,1,0:T(8,128)(2,1)}, bf16[5,64,1024]{2,1,0:T(8,128)(2,1)}, bf16[2,64,128]{2,1,0:T(8,128)(2,1)}) custom-call(bf16[32,64]{1,0:T(8,128)(2,1)} %bitcast.4, bf16[64,10240]{1,0:T(8,128)(2,1)} %fine_ref.3, s32[80,128]{1,0:T(8,128)} %nbr_ref.3, s32[64,128]{1,0:T(8,128)} %clinks_ref.3), custom_call_target="tpu_custom_call" | custom-call | tf_op jit(solution)/shard_map/coarse_gather/pallas_call | solution.py:226
  34.6 8.6 %blocks.1 = (bf16[64,10240]{1,0:T(8,128)(2,1)}, f32[64,10240]{1,0:T(8,128)}, bf16[32,64]{1,0:T(8,128)(2,1)}, bf16[5,64,1024]{2,1,0:T(8,128)(2,1)}, bf16[5,64,102...) custom-call(bf16[5,64,1024]{2,1,0:T(8,128)(2,1)} %get-tuple-element.17.near_ref, ...), custom_call_target="tpu_custom_call" | custom-call | tf_op jit(solution)/shard_map/blocks/pallas_call | solution.py:564
  43.2 27.4 %coarse_sum.1 = (f32[32,64]{1,0:T(8,128)}, f32[64,10240]{1,0:T(8,128)}, bf16[64,1024]{1,0:T(8,128)(2,1)}) custom-call(bf16[5,64,1024]{2,1,0:T(8,128)(2,1)} %get-tuple-element.21.terms_ref, bf16[5,64,1024]{2,1,0:T(8,128)(2,1)} %get-tuple-element.22.fterms_ref, bf16[64,128]{1,0:T(8,128)(2,1)} %get-tuple-element.23.extra_ref, ...), custom_call_target="tpu_custom_call" | custom-call | tf_op jit(solution)/shard_map/coarse_sum/pallas_call | solution.py:438
  70.7 0.0 copy-start
  70.7 3.5 %add_rim.1 = f32[64,10240]{1,0:T(8,128)} custom-call(f32[64,10240]{1,0:T(8,128)} %get-tuple-element.26.fine_ref, bf16[64,1024]{1,0:T(8,128)(2,1)} %get-tuple-element.27.rim_ref), custom_call_target="tpu_custom_call" | custom-call | tf_op jit(solution)/shard_map/add_rim/pallas_call | solution.py:613
  74.2 0.0 copy-done
  74.2 0.6 copy.13
Async XLA Ops:
  70.7 3.5 %copy-start = (f32[32,64]{1,0:T(8,128)S(1)}, f32[32,64]{1,0:T(8,128)}, u32[]{:S(2)}) copy-start(f32[32,64]{1,0:T(8,128)} %get-tuple-element.29) | copy-start | bytes 24580
